TPU v7x, 256 devices: a whole 4x4x8 slice. The times are simulated.
256 devices in a mesh: expert: 16 (over x_hi, y, core), blk: 16 (over x_lo, z).
Axes of the slice: x: 4 (x_hi: 2, x_lo: 2; x = x_hi * 2 + x_lo), y: 4, z: 8, core: 2. Of those that a mesh axis runs over, the one named last changes fastest.
Arguments:
- tokens: bfloat16 [2048, 6144], P(('expert', 'blk')), may hold values from -6 to 6
- out_grad: bfloat16 [2048, 6144], P(('expert', 'blk')), may hold values from -6 to 6
- expert_ids: int32 [2048, 4], P(('expert', 'blk')), may hold values from 0 to 15, as said below
- slots: int32 [2048, 4], P(('expert', 'blk')), may hold values from 0 to 2, as said below
- gates: bfloat16 [2048, 4], P(('expert', 'blk')), may hold values from 0.099609375 to 0.59765625
- w_in: bfloat16 [16, 5376, 6144], P('expert', 'blk'), may hold values from -0.078125 to 0.078125
- w_down: bfloat16 [16, 5376, 6144], P('expert', 'blk'), may hold values from -0.078125 to 0.078125
Outputs:
- grad_tokens: bfloat16 [2048, 6144], P(('expert', 'blk'))
- grad_gates: bfloat16 [2048, 4], P(('expert', 'blk'))
Inputs may be any that keep to these rules, and one draw needn't show every extreme that they name: `expert_ids`: within the 8 tokens of one device, a token names 4 different experts, no expert is named more than 3 times, and one expert is named exactly 3 times by every device. Among the entries of one device that name one expert, the slots are 0 to their count minus 1, each once.
All inputs are finite; a program needn't handle non-finite values.
Results may differ from a plain program's by a relative error of at most 0.019.
Values may be sent and summed in bfloat16 or wider, within the bound.
A program may use at most 128 MiB of HBM per device.

v0:
```python
import jax
import jax.numpy as jnp
from jax import lax
from jax.sharding import PartitionSpec as P


def hidden_terms(rows_x, rows_dy, rows_gate, weight_in, weight_down):
    contract = (((1,), (1,)), ((), ()))
    pre = lax.dot_general(rows_x, weight_in, contract, preferred_element_type=jnp.float32)
    back = lax.dot_general(rows_dy, weight_down, contract, preferred_element_type=jnp.float32)
    sigma = jax.nn.sigmoid(pre)
    gate_part = jnp.sum(pre * sigma * back, axis=1)
    slope = rows_gate.astype(jnp.float32)[:, None] * back * sigma * (1.0 + pre * (1.0 - sigma))
    return (slope.astype(jnp.bfloat16), gate_part)


def per_device(tokens, out_grad, expert_ids, slots, gates, w_in, w_down):
    tok_count = tokens.shape[0]
    top_count = expert_ids.shape[1]
    expert_count = lax.axis_size("expert")
    capacity = max(2, (tok_count * top_count + expert_count - 1) // expert_count + 1)
    slot_count = expert_count * capacity
    target = expert_ids * capacity + slots
    matches = (target[None, :, :] == jnp.arange(slot_count, dtype=jnp.int32)[:, None, None]).astype(
        jnp.float32
    )
    placing = jnp.sum(matches, axis=2).astype(jnp.bfloat16)
    send_x = jnp.dot(placing, tokens, preferred_element_type=jnp.float32).astype(jnp.bfloat16)
    send_dy = jnp.dot(placing, out_grad, preferred_element_type=jnp.float32).astype(jnp.bfloat16)
    send_gate = jnp.einsum("stk,tk->s", matches, gates.astype(jnp.float32)).astype(jnp.bfloat16)
    recv_x, recv_dy, recv_gate = (
        lax.all_to_all(send_x, "expert", split_axis=0, concat_axis=0, tiled=True),
        lax.all_to_all(send_dy, "expert", split_axis=0, concat_axis=0, tiled=True),
        lax.all_to_all(send_gate, "expert", split_axis=0, concat_axis=0, tiled=True),
    )
    weight_in = w_in[0]
    weight_down = w_down[0]
    all_x, all_dy, all_gate = (
        lax.all_gather(recv_x, "blk", axis=0, tiled=True),
        lax.all_gather(recv_dy, "blk", axis=0, tiled=True),
        lax.all_gather(recv_gate, "blk", axis=0, tiled=True),
    )
    slope, gate_part = hidden_terms(all_x, all_dy, all_gate, weight_in, weight_down)
    grad_rows = lax.psum_scatter(
        jnp.dot(slope, weight_in, preferred_element_type=jnp.float32).astype(jnp.bfloat16),
        "blk",
        scatter_dimension=0,
        tiled=True,
    )
    gate_rows = lax.psum_scatter(gate_part, "blk", scatter_dimension=0, tiled=True)
    back_rows, back_gate = (
        lax.all_to_all(grad_rows, "expert", split_axis=0, concat_axis=0, tiled=True),
        lax.all_to_all(
            gate_rows.astype(jnp.bfloat16), "expert", split_axis=0, concat_axis=0, tiled=True
        ),
    )
    grad_tokens = lax.dot_general(
        placing, back_rows, (((0,), (0,)), ((), ())), preferred_element_type=jnp.float32
    ).astype(jnp.bfloat16)
    grad_gates = jnp.einsum("stk,s->tk", matches, back_gate.astype(jnp.float32)).astype(
        jnp.bfloat16
    )
    return (grad_tokens, grad_gates)


def solution(mesh):
    return jax.shard_map(
        per_device,
        mesh=mesh,
        in_specs=(
            P(("expert", "blk"), None),
            P(("expert", "blk"), None),
            P(("expert", "blk"), None),
            P(("expert", "blk"), None),
            P(("expert", "blk"), None),
            P("expert", "blk", None),
            P("expert", "blk", None),
        ),
        out_specs=(P(("expert", "blk"), None), P(("expert", "blk"), None)),
        check_vma=False,
    )
```

profile of v0, /device:TPU:1, one launch (start us, length us, event | category | flops | bytes accessed | tf_op | source)
XLA Modules:
  0.0 417.5 jit_solution(10140539445193351380)
XLA Ops:
  7.2 0.0 copy-start
  7.2 0.0 copy-start.2
  7.2 0.0 all-gather.5.cloned.1.call-start
  7.2 0.7 multiply_add_fusion
  8.0 0.1 convert_reduce_fusion
  8.1 0.0 copy-done
  8.1 0.3 convolution_convert_fusion.1
  8.4 0.4 all_to_all.46
  8.8 22.5 %all_to_all.62 = bf16[16,3,6144]{2,1,0:T(4,128)(2,1)S(1)} all-to-all(bf16[16,3,6144]{2,1,0:T(4,128)(2,1)S(1)} %all_to_all.46), channel_id=1, replica_groups=mesh['expert'=16,'blk'=16] {'expert'}, dimensions={0} | all-to-all | bytes 1179648 | tf_op jit(solution)/shard_map/all_to_all | solution.py:32
  31.4 0.0 copy-start.4
  31.4 0.0 copy-start.3
  31.4 1.2 all_to_all.48
  32.6 0.0 all-gather.5.cloned.1.call-update
  32.6 0.0 all-gather.3.cloned.1.call-start
  32.7 0.0 copy-done.2
  32.7 0.3 convolution_convert_fusion.2
  33.0 0.4 all_to_all.43
  33.4 17.8 %all_to_all.63 = bf16[16,3,6144]{2,1,0:T(4,128)(2,1)S(1)} all-to-all(bf16[16,3,6144]{2,1,0:T(4,128)(2,1)S(1)} %all_to_all.43), channel_id=1, replica_groups=mesh['expert'=16,'blk'=16] {'expert'}, dimensions={0} | all-to-all | bytes 1179648 | tf_op jit(solution)/shard_map/all_to_all | solution.py:33
  51.2 1.2 all_to_all.45
  52.4 0.0 all-gather.3.cloned.1.call-update
  52.5 0.0 copy-done.4
  52.5 0.2 fusion.5
  52.7 0.7 all_to_all.55
  53.4 99.0 %all-to-all-start = ((bf16[16,3,1]{1,2,0:T(2,128)(2,1)}), bf16[16,3,1]{1,2,0:T(2,128)(2,1)S(1)}, u32[]{:S(2)}, u32[]{:S(2)}) async-start(bf16[16,3,1]{1,2,0:T(2,128)(2,1)} %all_to_all.55), calls=%async_computation | async-start | bytes 16384 | tf_op jit(solution)/shard_map/all_to_all | solution.py:34
  152.4 0.0 reduce-scatter.2.cloned.1.call-start
  152.5 0.0 copy-done.3
  152.5 0.6 fusion.16
  153.6 5.8 %all-to-all-done = bf16[16,3,1]{1,2,0:T(2,128)(2,1)S(1)} async-done(((bf16[16,3,1]{1,2,0:T(2,128)(2,1)}), bf16[16,3,1]{1,2,0:T(2,128)(2,1)S(1)}, u32[]{:S(2)}, u32[]{:S(2)}) %all-to-all-start) | async-done | bytes 128 | tf_op jit(solution)/shard_map/all_to_all | solution.py:34
  159.4 0.1 reshape.16
  159.6 0.2 dynamic-update-slice
  159.8 32.6 %all-reduce = bf16[768]{0:T(1024)(128)(2,1)S(1)} all-reduce(bf16[768]{0:T(1024)(128)(2,1)S(1)} %dynamic-update-slice), channel_id=1, replica_groups=mesh['expert'=16,'blk'=16] {'blk'}, use_global_device_ids=true, to_apply=%add | all-reduce | flops 768 | bytes 3072
  192.4 0.0 all-gather.5.cloned.1.call-done
  192.4 11.0 %fusion.1 = f32[768,336]{0,1:T(8,128)S(1)} fusion(bf16[768,6144]{1,0:T(8,128)(2,1)} %all-gather.5.cloned.1.call-done, bf16[1,336,6144]{2,1,0:T(8,128)(2,1)} %param.12), kind=kOutput, calls=%fused_computation.5 | convolution fusion | flops 3170893824 | bytes 14598144 | tf_op jit(solution)/shard_map/dot_general | solution.py:9
  203.4 53.5 %all-gather.3.cloned.1.call-done = bf16[768,6144]{1,0:T(8,128)(2,1)} async-done(((bf16[48,6144]{1,0:T(8,128)(2,1)}), bf16[768,6144]{1,0:T(8,128)(2,1)}) %all-gather.3.cloned.1.call-update) | async-done | bytes 9437200 | tf_op jit(solution)/shard_map/all_gather | solution.py:40
  257.0 0.0 copy-start.1
  257.0 11.0 %multiply_reduce_fusion = (f32[768]{0:T(1024)S(1)}, f32[768,336]{0,1:T(8,128)S(1)}) fusion(f32[768,336]{0,1:T(8,128)S(1)} %fusion.1, bf16[768,6144]{1,0:T(8,128)(2,1)} %all-gather.3.cloned.1.call-done, bf16[1,336,6144]{2,1,0:T(8,128)(2,1)} %param.13), kind=kOutput, calls=%fused_computation.11 | convolution fusion | flops 3172441344 | bytes 15633408 | tf_op jit(solution)/shard_map/dot_general | solution.py:10
  268.0 0.0 copy-done.1
  268.0 8.0 %convolution_convert_fusion = bf16[768,6144]{1,0:T(8,128)(2,1)} fusion(bf16[1,336,6144]{2,1,0:T(8,128)(2,1)S(1)} %copy-done.1, f32[768,336]{0,1:T(8,128)S(1)} %fusion.1, f32[768,336]{0,1:T(8,128)S(1)} %get-tuple-element.5, f32[768]{0:T(1024)S(1)} %convert_element_type.38), kind=kOutput, calls=%fused_computation | convolution fusion | flops 3178192896 | bytes 15633408 | tf_op jit(solution)/shard_map/dot_general | solution.py:45
  276.0 0.0 reduce-scatter.2.cloned.1.call-update
  276.7 27.5 %all-reduce.1 = bf16[768]{0:T(1024)(128)(2,1)S(1)} all-reduce(f32[768]{0:T(1024)S(1)} %get-tuple-element.4), channel_id=3, replica_groups=mesh['expert'=16,'blk'=16] {'blk'}, use_global_device_ids=true, to_apply=%region_3.0.clone | all-reduce | flops 768 | bytes 4608
  304.2 0.1 dynamic-slice.4
  304.3 0.7 all_to_all.56
  305.0 12.2 %all-to-all-start.4 = ((bf16[16,3,1]{1,2,0:T(2,128)(2,1)}), bf16[16,3,1]{1,2,0:T(2,128)(2,1)S(1)}, u32[]{:S(2)}, u32[]{:S(2)}) async-start(bf16[16,3,1]{1,2,0:T(2,128)(2,1)} %all_to_all.56), calls=%async_computation.5 | async-start | bytes 16384 | tf_op jit(solution)/shard_map/all_to_all | solution.py:53
  317.2 68.8 %reduce-scatter.2.cloned.1.call-done = bf16[48,6144]{1,0:T(8,128)(2,1)} async-done(((bf16[768,6144]{1,0:T(8,128)(2,1)}), bf16[48,6144]{1,0:T(8,128)(2,1)}) %reduce-scatter.2.cloned.1.call-update) | async-done | bytes 589840 | tf_op jit(solution)/shard_map/reduce_scatter | solution.py:44
  386.0 2.1 all_to_all.49
  388.1 0.0 all-to-all-done.4
  388.1 7.1 %all-to-all-start.3 = ((bf16[16,3,6144]{2,1,0:T(4,128)(2,1)}), bf16[16,3,6144]{2,1,0:T(4,128)(2,1)S(1)}, u32[]{:S(2)}, u32[]{:S(2)}) async-start(bf16[16,3,6144]{2,1,0:T(4,128)(2,1)} %all_to_all.49), calls=%async_computation.4 | async-start | bytes 1572864 | tf_op jit(solution)/shard_map/all_to_all | solution.py:52
  395.2 0.1 reshape.23
  395.3 0.2 fusion.8
  395.5 0.6 convert_element_type.45
  396.1 13.5 %all-to-all-done.3 = bf16[16,3,6144]{2,1,0:T(4,128)(2,1)S(1)} async-done(((bf16[16,3,6144]{2,1,0:T(4,128)(2,1)}), bf16[16,3,6144]{2,1,0:T(4,128)(2,1)S(1)}, u32[]{:S(2)}, u32[]{:S(2)}) %all-to-all-start.3) | async-done | bytes 589856 | tf_op jit(solution)/shard_map/all_to_all | solution.py:52
  409.6 0.5 all_to_all.51
  410.1 0.8 convolution_convert_fusion.3
  (4 shorter events, 0.1 us)
Async XLA Ops:
  7.2 0.9 copy-start
  7.2 25.5 %copy-start.2 = (bf16[8,6144]{1,0:T(8,128)(2,1)S(1)}, bf16[8,6144]{1,0:T(8,128)(2,1)}, u32[]{:S(2)}) copy-start(bf16[8,6144]{1,0:T(8,128)(2,1)} %param.8) | copy-start | bytes 294916
  7.2 185.2 %all-gather.5.cloned.1.call-start = ((), (), s32[]{:S(2)}) async-start(), calls=%async_computation.7 | async-start | bytes 10027008 | tf_op jit(solution)/shard_map/all_gather | solution.py:39
  31.4 21.1 %copy-start.4 = (bf16[8,4]{0,1:T(4,128)(2,1)S(1)}, bf16[8,4]{0,1:T(4,128)(2,1)}, u32[]{:S(2)}) copy-start(bf16[8,4]{0,1:T(4,128)(2,1)} %param.11) | copy-start | bytes 196
  31.4 121.1 %copy-start.3 = (u32[256]{0:T(256)S(1)}, u32[256]{0:T(256)}, u32[]{:S(2)}) copy-start(u32[256]{0:T(256)} %constant.15) | copy-start | bytes 3076
  32.6 224.3 %all-gather.3.cloned.1.call-start = ((), (), s32[]{:S(2)}) async-start(), calls=%async_computation.6 | async-start | bytes 10027008 | tf_op jit(solution)/shard_map/all_gather | solution.py:40
  53.4 106.0 %all-to-all-start = ((bf16[16,3,1]{1,2,0:T(2,128)(2,1)}), bf16[16,3,1]{1,2,0:T(2,128)(2,1)S(1)}, u32[]{:S(2)}, u32[]{:S(2)}) async-start(bf16[16,3,1]{1,2,0:T(2,128)(2,1)} %all_to_all.55), calls=%async_computation | async-start | bytes 16384 | tf_op jit(solution)/shard_map/all_to_all | solution.py:34
  152.4 233.6 %reduce-scatter.2.cloned.1.call-start = ((), (), s32[]{:S(2)}) async-start(), calls=%async_computation.8 | async-start | bytes 10027008 | tf_op jit(solution)/shard_map/reduce_scatter | solution.py:44
  257.0 11.0 %copy-start.1 = (bf16[1,336,6144]{2,1,0:T(8,128)(2,1)S(1)}, bf16[1,336,6144]{2,1,0:T(8,128)(2,1)}, u32[]{:S(2)}) copy-start(bf16[1,336,6144]{2,1,0:T(8,128)(2,1)} %param.12) | copy-start | bytes 12386308
  305.0 83.1 %all-to-all-start.4 = ((bf16[16,3,1]{1,2,0:T(2,128)(2,1)}), bf16[16,3,1]{1,2,0:T(2,128)(2,1)S(1)}, u32[]{:S(2)}, u32[]{:S(2)}) async-start(bf16[16,3,1]{1,2,0:T(2,128)(2,1)} %all_to_all.56), calls=%async_computation.5 | async-start | bytes 16384 | tf_op jit(solution)/shard_map/all_to_all | solution.py:53
  388.1 21.5 %all-to-all-start.3 = ((bf16[16,3,6144]{2,1,0:T(4,128)(2,1)}), bf16[16,3,6144]{2,1,0:T(4,128)(2,1)S(1)}, u32[]{:S(2)}, u32[]{:S(2)}) async-start(bf16[16,3,6144]{2,1,0:T(4,128)(2,1)} %all_to_all.49), calls=%async_computation.4 | async-start | bytes 1572864 | tf_op jit(solution)/shard_map/all_to_all | solution.py:52
Sparse Core Ops, SparseCore 0:
  32.7 110.5 all-gather.4
  145.1 111.8 all-gather.2
  276.2 109.7 reduce-scatter.1
where the time goes:
time: 418 us; the launch traced here: 417 us
  waiting for transfers between devices  142 us (34%)
  starting transfers between devices  118 us (28%)
  blocking collectives  100 us (24%)
  matrix products  32 us (8%)
  between operations  15.1 us (4%)
  local copies, waits for them, and re-layouts  8.4 us (2%)
    all_to_all x1, starting transfers between devices, per_device(): lax.all_to_all(send_gate, 'expert', split_axis=0, concat_axis=0, tiled=True)  99 us
    reduce_scatter x1, waiting for transfers between devices, per_device(): lax.psum_scatter(jnp.dot(slope, weight_in, preferred_element_type=jnp.flo...  68.8 us
    unnamed x2, blocking collectives  60.1 us
    all_gather x1, waiting for transfers between devices, per_device(): lax.all_gather(recv_dy, 'blk', axis=0, tiled=True)  53.5 us
    all_to_all x1, blocking collectives, per_device(): lax.all_to_all(send_x, 'expert', split_axis=0, concat_axis=0, tiled=True)  22.5 us
    all_to_all x1, blocking collectives, per_device(): lax.all_to_all(send_dy, 'expert', split_axis=0, concat_axis=0, tiled=True)  17.8 us
    all_to_all x1, waiting for transfers between devices, per_device(): lax.all_to_all(grad_rows, 'expert', split_axis=0, concat_axis=0, tiled=True)  13.5 us
    all_to_all x1, starting transfers between devices, per_device(): lax.all_to_all(gate_rows.astype(jnp.bfloat16), 'expert', split_axis=0, co...  12.2 us
  transfers between devices with their start and end apart: 6, of which 4 were waited for; matrix products, arithmetic and copies ran while one was open for 3% of the time, Pallas kernels for 0%

commit v1 on v0

v1 whole, which is shorter than its diff:
```python
import functools

import jax
import jax.numpy as jnp
from jax import lax
from jax.experimental import pallas as pl
from jax.experimental.pallas import tpu as pltpu
from jax.sharding import PartitionSpec as P

MESH = pl.DeviceIdType.MESH
RING = 8
LANES = 128


def nt(a, b):
    return lax.dot_general(a, b, (((1,), (1,)), ((), ())), preferred_element_type=jnp.float32)


def kernel(
    rows_ref, win_ref, wdn_ref, out_ref,
    X, WI, WD, PRE, BACK, ES, ER, SL, PART, SU, SD, RU, RD,
    loc_sem, ws_sem, wr_sem, us_sem, ur_sem, ds_sem, dr_sem, es_sem, er_sem,
    rus_sem, rur_sem, rds_sem, rdr_sem,
):
    R, half = rows_ref.shape[0], rows_ref.shape[1] // 2
    U = R // 2
    blk = lax.axis_index("blk")
    xl, z = blk // RING, blk % RING
    above = {"blk": xl * RING + (z + 1) % RING}
    below = {"blk": xl * RING + (z + RING - 1) % RING}
    pair = {"blk": (1 - xl) * RING + z}

    barrier = pltpu.get_barrier_semaphore()
    for peer in (above, below, pair):
        pl.semaphore_signal(barrier, inc=1, device_id=peer, device_id_type=MESH)

    mine = pl.ds(pl.multiple_of(xl * half, LANES), half)
    theirs = pl.ds(pl.multiple_of((1 - xl) * half, LANES), half)
    local = [
        pltpu.make_async_copy(rows_ref, X.at[0, pl.ds(R, R), :], loc_sem.at[0]),
        pltpu.make_async_copy(win_ref.at[:, mine], WI.at[xl], loc_sem.at[1]),
        pltpu.make_async_copy(wdn_ref.at[:, mine], WD.at[xl], loc_sem.at[2]),
    ]
    for c in local:
        c.start()

    def remote(src, dst, ss, rs, peer):
        return pltpu.make_async_remote_copy(
            src_ref=src, dst_ref=dst, send_sem=ss, recv_sem=rs, device_id=peer, device_id_type=MESH
        )

    pl.semaphore_wait(barrier, 3)

    weights_out = [
        remote(win_ref.at[:, theirs], WI.at[xl], ws_sem.at[0], wr_sem.at[0], pair),
        remote(wdn_ref.at[:, theirs], WD.at[xl], ws_sem.at[1], wr_sem.at[1], pair),
    ]
    for c in weights_out:
        c.start()

    def up(s, u):
        src = X.at[0, pl.ds(R + u * U, U), :] if s == 1 else X.at[s - 1, pl.ds(u * U, U), :]
        dst = X.at[s % 4, pl.ds(u * U, U), :]
        return remote(src, dst, us_sem.at[s - 1, u], ur_sem.at[s - 1, u], above)

    def down(s, u):
        src = X.at[(s - 1) % 4, pl.ds(R + u * U, U), :]
        dst = X.at[s, pl.ds(R + u * U, U), :] if s < 4 else X.at[0, pl.ds(u * U, U), :]
        return remote(src, dst, ds_sem.at[s - 1, u], dr_sem.at[s - 1, u], below)

    local[0].wait()
    for u in range(2):
        up(1, u).start()
        down(1, u).start()
    local[1].wait()
    local[2].wait()

    def project(q, h):
        PRE[q, h] = nt(X[q, :, :half], WI[h])
        BACK[q, h] = nt(X[q, :, half:], WD[h])

    for s in range(1, 4):
        for u in range(2):
            up(s, u).wait_recv()
            if s < 3 or u == 0:
                up(s + 1, u).start()
            down(s, u).wait_recv()
            if s < 3 or u == 1:
                down(s + 1, u).start()
        project(s, xl)
    up(4, 0).wait_recv()
    down(4, 1).wait_recv()
    project(0, xl)
    remote(win_ref.at[:, mine], WI.at[1 - xl], ws_sem.at[0], wr_sem.at[0], pair).wait_recv()
    remote(wdn_ref.at[:, mine], WD.at[1 - xl], ws_sem.at[1], wr_sem.at[1], pair).wait_recv()

    def swap(k):
        q, at, n = ((0, 0, R), (3, 0, 2 * R), (2, 0, 2 * R), (1, 0, 2 * R), (0, R, R))[k]
        there = (q, slice(None), slice(None), pl.ds(at, n), slice(None))
        return remote(ES.at[there], ER.at[there], es_sem.at[k], er_sem.at[k], pair)

    def project_and_send(k):
        q = (0, 3, 2, 1)[k]
        project(q, 1 - xl)
        for h in range(2):
            ES[q, 0, h] = PRE[q, h].astype(jnp.bfloat16)
            ES[q, 1, h] = BACK[q, h].astype(jnp.bfloat16)
        swap(k).start()
        if k == 3:
            swap(4).start()

    def terms(k):
        q, at, n = ((0, 0, R), (3, 0, 2 * R), (2, 0, 2 * R), (1, 0, 2 * R), (0, R, R))[k]
        rows = pl.ds(at, n)
        swap(k).wait_recv()
        gate = jnp.zeros((n, 1), jnp.float32)
        for h in range(2):
            pre = PRE[q, h, rows, :] + ER[q, 0, h, rows, :].astype(jnp.float32)
            back = BACK[q, h, rows, :] + ER[q, 1, h, rows, :].astype(jnp.float32)
            sigma = jax.nn.sigmoid(pre)
            act = pre * sigma
            gate = gate + jnp.sum(act * back, axis=1, keepdims=True)
            SL[h, rows, :] = (back * sigma * (1.0 + pre * (1.0 - sigma))).astype(jnp.bfloat16)
        PART[rows, pl.ds(half, LANES)] = jnp.broadcast_to(gate, (n, LANES))
        step = 4 * LANES

        def columns(c, carry):
            there = pl.ds(pl.multiple_of(c * step, step), step)
            PART[rows, there] = jnp.dot(
                SL[0, rows, :], WI[0, :, there], preferred_element_type=jnp.float32
            ) + jnp.dot(SL[1, rows, :], WI[1, :, there], preferred_element_type=jnp.float32)
            return carry

        lax.fori_loop(0, half // step, columns, 0)

    def sum_up(i, u):
        rows = pl.ds(u * U, U)
        return remote(SU.at[i, rows, :], RU.at[i, rows, :], rus_sem.at[i, u], rur_sem.at[i, u], above)

    def sum_down(i, u):
        rows = pl.ds(u * U, U)
        return remote(SD.at[i, rows, :], RD.at[i, rows, :], rds_sem.at[i, u], rdr_sem.at[i, u], below)

    project_and_send(0)
    project_and_send(1)
    terms(0)
    SU[0, 0:U, :] = PART[0:U, :].astype(jnp.bfloat16)
    sum_up(0, 0).start()
    SD[0, U:R, :] = PART[U:R, :].astype(jnp.bfloat16)
    sum_down(0, 1).start()
    for k in range(1, 4):
        if k < 3:
            project_and_send(k + 1)
        terms(k)
        for u in range(2):
            own = slice(u * U, u * U + U)
            term = PART[R + u * U : R + u * U + U, :]
            if k > 1 or u == 0:
                sum_up(k - 1, u).wait_recv()
                term = term + RU[k - 1, own, :].astype(jnp.float32)
            SU[k, own, :] = term.astype(jnp.bfloat16)
            sum_up(k, u).start()
            term = PART[own, :]
            if k > 1 or u == 1:
                sum_down(k - 1, u).wait_recv()
                term = term + RD[k - 1, own, :].astype(jnp.float32)
            SD[k, own, :] = term.astype(jnp.bfloat16)
            sum_down(k, u).start()
    terms(4)
    for u in range(2):
        own = slice(u * U, u * U + U)
        sum_up(3, u).wait_recv()
        sum_down(3, u).wait_recv()
        out_ref[own, :] = (
            PART[R + u * U : R + u * U + U, :]
            + RU[3, own, :].astype(jnp.float32)
            + RD[3, own, :].astype(jnp.float32)
        ).astype(out_ref.dtype)

    for c in weights_out:
        c.wait_send()
    for s in range(1, 5):
        for u in range(2):
            if s < 4 or u == 0:
                up(s, u).wait_send()
            if s < 4 or u == 1:
                down(s, u).wait_send()
    for k in range(5):
        swap(k).wait_send()
    for i in range(4):
        for u in range(2):
            if i > 0 or u == 0:
                sum_up(i, u).wait_send()
            if i > 0 or u == 1:
                sum_down(i, u).wait_send()


def expert_rows(rows, w_in, w_down):
    n_rows, width = rows.shape
    half, hidden = width // 2, w_in.shape[0]
    wide = half + LANES
    bf16, f32, dma = jnp.bfloat16, jnp.float32, pltpu.SemaphoreType.DMA
    return pl.pallas_call(
        kernel,
        out_shape=jax.ShapeDtypeStruct((n_rows, wide), bf16),
        in_specs=[pl.BlockSpec(memory_space=pl.ANY)] * 3,
        out_specs=pl.BlockSpec(memory_space=pltpu.VMEM),
        scratch_shapes=[
            pltpu.VMEM((4, 2 * n_rows, width), bf16),
            pltpu.VMEM((2, hidden, half), bf16),
            pltpu.VMEM((2, hidden, half), bf16),
            pltpu.VMEM((4, 2, 2 * n_rows, hidden), f32),
            pltpu.VMEM((4, 2, 2 * n_rows, hidden), f32),
            pltpu.VMEM((4, 2, 2, 2 * n_rows, hidden), bf16),
            pltpu.VMEM((4, 2, 2, 2 * n_rows, hidden), bf16),
            pltpu.VMEM((2, 2 * n_rows, hidden), bf16),
            pltpu.VMEM((2 * n_rows, wide), f32),
            pltpu.VMEM((4, n_rows, wide), bf16),
            pltpu.VMEM((4, n_rows, wide), bf16),
            pltpu.VMEM((4, n_rows, wide), bf16),
            pltpu.VMEM((4, n_rows, wide), bf16),
            dma((3,)), dma((2,)), dma((2,)),
            dma((4, 2)), dma((4, 2)), dma((4, 2)), dma((4, 2)),
            dma((5,)), dma((5,)),
            dma((4, 2)), dma((4, 2)), dma((4, 2)), dma((4, 2)),
        ],
        compiler_params=pltpu.CompilerParams(
            collective_id=0, has_side_effects=True, vmem_limit_bytes=60 * 2**20
        ),
    )(rows, w_in, w_down)


def per_device(tokens, out_grad, expert_ids, slots, gates, w_in, w_down):
    tok_count, width = tokens.shape
    half = width // 2
    top_count = expert_ids.shape[1]
    expert_count, blk_count = lax.axis_size("expert"), lax.axis_size("blk")
    capacity = max(2, (tok_count * top_count + expert_count - 1) // expert_count + 1)
    swap = [(i, (i + RING) % blk_count) for i in range(blk_count)]
    xl = lax.axis_index("blk") // RING

    def cut(a, side):
        return lax.dynamic_slice(a, (0, side * half), (tok_count, half))

    small = jnp.concatenate(
        [(expert_ids * (2 * capacity) + slots + capacity * xl).astype(jnp.bfloat16), gates], axis=1
    )
    small = jnp.pad(small, ((0, 0), (0, LANES - 2 * top_count)))
    away = jnp.concatenate([cut(tokens, 1 - xl), cut(out_grad, 1 - xl), small], axis=1)
    stay = jnp.concatenate([cut(tokens, xl), cut(out_grad, xl), small], axis=1)
    came = lax.ppermute(away, "blk", swap)
    both = jnp.concatenate([stay, came], axis=0)
    target = both[:, width : width + top_count].astype(jnp.int32)
    weight = both[:, width + top_count : width + 2 * top_count].astype(jnp.float32)
    slot_count = expert_count * 2 * capacity
    matches = (target[None] == jnp.arange(slot_count, dtype=jnp.int32)[:, None, None]).astype(
        jnp.float32
    )
    placing = jnp.sum(matches, axis=2).astype(jnp.bfloat16)
    weighed = jnp.sum(matches * weight[None], axis=2).astype(jnp.bfloat16)
    send = jnp.dot(placing, both[:, :width], preferred_element_type=jnp.float32).astype(jnp.bfloat16)
    rows = lax.all_to_all(send, "expert", split_axis=0, concat_axis=0, tiled=True)
    grads = expert_rows(rows, w_in[0], w_down[0])
    back = lax.all_to_all(grads, "expert", split_axis=0, concat_axis=0, tiled=True)
    grad = lax.dot_general(
        weighed, back[:, :half], (((0,), (0,)), ((), ())), preferred_element_type=jnp.float32
    ).astype(jnp.bfloat16)
    own, other = grad[:tok_count], grad[tok_count:]
    other = lax.ppermute(other, "blk", swap)
    grad_tokens = jnp.where(
        xl == 0, jnp.concatenate([own, other], axis=1), jnp.concatenate([other, own], axis=1)
    )
    grad_gates = jnp.einsum(
        "stk,s->tk", matches[:, :tok_count], back[:, half].astype(jnp.float32)
    ).astype(jnp.bfloat16)
    return (grad_tokens, grad_gates)


def solution(mesh):
    return jax.shard_map(
        per_device,
        mesh=mesh,
        in_specs=(
            P(("expert", "blk"), None),
            P(("expert", "blk"), None),
            P(("expert", "blk"), None),
            P(("expert", "blk"), None),
            P(("expert", "blk"), None),
            P("expert", "blk", None),
            P("expert", "blk", None),
        ),
        out_specs=(P(("expert", "blk"), None), P(("expert", "blk"), None)),
        check_vma=False,
    )
```

time: 418 us -> 235 us (0.56)
  Pallas kernels: 0 us -> 157 us
  waiting for transfers between devices: 142 us -> 17.5 us
  starting transfers between devices: 118 us -> 16.9 us
  blocking collectives: 100 us -> 31.3 us
  matrix products: 32 us -> 0.8 us
  between operations: 15.1 us -> 0.72 us
    pallas_call x0 -> x1, Pallas kernels: none -> 157 us  [expert_rows(): pl.pallas_call(kernel, out_shape=jax.ShapeDtypeStruct((n_rows, wide), bf1...]
    all_to_all x3 -> x1, starting transfers between devices: 118 us -> 12.9 us  [per_device(): lax.all_to_all(grads, 'expert', split_axis=0, concat_axis=0, tiled=True)]
    reduce_scatter x1 -> x0, waiting for transfers between devices: 68.8 us -> none  [per_device(): lax.psum_scatter(jnp.dot(slope, weight_in, preferred_element_type=jnp.flo...]
    unnamed x2 -> x0, blocking collectives: 60.1 us -> none
    all_gather x2 -> x0, waiting for transfers between devices: 53.6 us -> none  [the longest x1 53.5 us: per_device(): lax.all_gather(recv_dy, 'blk', axis=0, tiled=True)]
    dot_general x8 -> x3, matrix products: 32 us -> 0.8 us  [the longest x1 0.49 us: per_device(): jnp.dot(placing, both[:, :width], preferred_element_type=jnp.float32)]
    all_to_all x2 -> x1, blocking collectives: 40.3 us -> 31.3 us  [per_device(): lax.all_to_all(send, 'expert', split_axis=0, concat_axis=0, tiled=True)]
    all_to_all x3 -> x1, waiting for transfers between devices: 19.2 us -> 14.7 us  [per_device(): lax.all_to_all(grads, 'expert', split_axis=0, concat_axis=0, tiled=True)]
  transfers between devices with their start and end apart: 6 -> 3, of which waited for: 4 -> 3; matrix products, arithmetic and copies ran while one was open for 3% -> 0% of each run, Pallas kernels for 0% -> 0%
where the time goes in v1:
time: 235 us; the launch traced here: 234 us
  Pallas kernels  157 us (67%)
  blocking collectives  31.3 us (13%)
  waiting for transfers between devices  17.5 us (7%)
  starting transfers between devices  16.9 us (7%)
  local copies, waits for them, and re-layouts  7.46 us (3%)
    pallas_call x1, Pallas kernels, expert_rows(): pl.pallas_call(kernel, out_shape=jax.ShapeDtypeStruct((n_rows, wide), bf1...  157 us
    all_to_all x1, blocking collectives, per_device(): lax.all_to_all(send, 'expert', split_axis=0, concat_axis=0, tiled=True)  31.3 us
    all_to_all x1, waiting for transfers between devices, per_device(): lax.all_to_all(grads, 'expert', split_axis=0, concat_axis=0, tiled=True)  14.7 us
    all_to_all x1, starting transfers between devices, per_device(): lax.all_to_all(grads, 'expert', split_axis=0, concat_axis=0, tiled=True)  12.9 us
  transfers between devices with their start and end apart: 3, of which 3 were waited for; matrix products, arithmetic and copies ran while one was open for 0% of the time, Pallas kernels for 0%

profile of v1, /device:TPU:1, one launch (start us, length us, event | category | flops | bytes accessed | tf_op | source)
XLA Modules:
  0.0 233.7 jit_solution(12725887632128002608)
XLA Ops:
  0.7 0.8 copy.24
  1.4 0.8 copy.25
  2.2 0.8 copy.26
  2.9 0.1 fusion.8
  3.0 0.9 constant_dynamic-slice_fusion.2
  3.9 2.1 collective-permute-start
  6.1 2.0 collective-permute-done
  8.1 0.1 pad_maximum_fusion.8
  8.2 0.1 copy.30
  8.3 0.1 copy.31
  8.4 0.1 select_reduce_fusion
  8.5 0.5 convolution_convert_fusion
  8.9 0.5 all_to_all.15
  9.4 31.3 %all_to_all.23 = bf16[16,6,6144]{2,1,0:T(8,128)(2,1)S(1)} all-to-all(bf16[16,6,6144]{2,1,0:T(8,128)(2,1)S(1)} %all_to_all.15), channel_id=1, replica_groups=mesh['expert'=16,'blk'=16] {'expert'}, dimensions={0} | all-to-all | bytes 2359296 | tf_op jit(solution)/shard_map/all_to_all | solution.py:262
  40.8 1.2 all_to_all.17.rows_ref
  42.0 157.4 %shard_map.86 = bf16[96,3200]{1,0:T(8,128)(2,1)} custom-call(bf16[96,6144]{1,0:T(8,128)(2,1)} %all_to_all.17.rows_ref, bf16[336,6144]{1,0:T(8,128)(2,1)} %bitcast.10, bf16[336,6144]{1,0:T(8,128)(2,1)} %bitcast.11), custom_call_target="tpu_custom_call" | custom-call | tf_op jit(solution)/shard_map/pallas_call | solution.py:203
  199.4 2.1 all_to_all.18
  201.5 12.9 %all-to-all-start.1 = ((bf16[16,6,3200]{2,1,0:T(8,128)(2,1)}), bf16[16,6,3200]{2,1,0:T(8,128)(2,1)S(1)}, u32[]{:S(2)}, u32[]{:S(2)}) async-start(bf16[16,6,3200]{2,1,0:T(8,128)(2,1)} %all_to_all.18), calls=%async_computation.1 | async-start | bytes 1638400 | tf_op jit(solution)/shard_map/all_to_all | solution.py:264
  214.4 0.1 iota_compare_fusion
  214.4 14.7 %all-to-all-done.1 = bf16[16,6,3200]{2,1,0:T(8,128)(2,1)S(1)} async-done(((bf16[16,6,3200]{2,1,0:T(8,128)(2,1)}), bf16[16,6,3200]{2,1,0:T(8,128)(2,1)S(1)}, u32[]{:S(2)}, u32[]{:S(2)}) %all-to-all-start.1) | async-done | bytes 614432 | tf_op jit(solution)/shard_map/all_to_all | solution.py:264
  229.1 0.2 all_to_all.20
  229.3 0.1 slice_reduce_fusion
  229.4 0.2 convolution_convert_fusion.1
  229.7 1.9 collective-permute-start.1
  231.6 0.1 fusion.2
  231.7 0.6 convert_element_type.38
  232.3 0.8 collective-permute-done.1
  233.1 0.7 maximum_select_fusion
  (5 shorter events, 0.1 us)
Async XLA Ops:
  3.9 4.2 %collective-permute-start = (bf16[8,6272]{1,0:T(8,128)(2,1)S(1)}, bf16[8,6272]{1,0:T(8,128)(2,1)S(1)}, u32[]{:S(2)}, u32[]{:S(2)}) collective-permute-start(bf16[8,6272]{1,0:T(8,128)(2,1)S(1)} %pad_maximum_fusion.6), channel_id=1, source_target_pairs={{0,8},{1,9},{2,10},{3,11},{4,12},{5,13},{6,14},{7,15},{8,0},{9,1},... | collective-permute-start | bytes 301064 | tf_op jit(solution)/shard_map/ppermute | solution.py:251
  201.5 27.6 %all-to-all-start.1 = ((bf16[16,6,3200]{2,1,0:T(8,128)(2,1)}), bf16[16,6,3200]{2,1,0:T(8,128)(2,1)S(1)}, u32[]{:S(2)}, u32[]{:S(2)}) async-start(bf16[16,6,3200]{2,1,0:T(8,128)(2,1)} %all_to_all.18), calls=%async_computation.1 | async-start | bytes 1638400 | tf_op jit(solution)/shard_map/all_to_all | solution.py:264
  229.7 3.4 %collective-permute-start.1 = (bf16[8,3072]{1,0:T(8,128)(2,1)S(1)}, bf16[8,3072]{1,0:T(8,128)(2,1)S(1)}, u32[]{:S(2)}, u32[]{:S(2)}) collective-permute-start(bf16[8,3072]{1,0:T(8,128)(2,1)S(1)} %get-tuple-element.7), channel_id=1, source_target_pairs={{0,8},{1,9},{2,10},{3,11},{4,12},{5,13},{6,14},{7,15},{8,0},{9,1},... | collective-permute-start | bytes 147464 | tf_op jit(solution)/shard_map/ppermute | solution.py:269

commit v2 on v0

v2 whole, which is shorter than its diff:
```python
import functools

import jax
import jax.numpy as jnp
from jax import lax
from jax.experimental import pallas as pl
from jax.experimental.pallas import tpu as pltpu
from jax.sharding import PartitionSpec as P

MESH = pl.DeviceIdType.MESH
RING = 8
LANES = 128


def nt(a, b):
    return lax.dot_general(a, b, (((1,), (1,)), ((), ())), preferred_element_type=jnp.float32)


GROUPS = ((3, 0), (0, 0), (2, 0), (3, 1), (1, 0), (2, 1), (1, 1), (0, 1))
BEFORE = (None, None, (0, False), (1, True), (2, False), (3, False), (5, False))
CHUNKS = 8


def kernel(
    send_ref, win_ref, wdn_ref, out_ref,
    GOT, X, WI, WD, PRE, BACK, ES, ER, SL, PART, SUM, ARR, MIX, TURN, TS,
    loc_sem, ws_sem, wr_sem, us_sem, ur_sem, ds_sem, dr_sem, es_sem, er_sem,
    ss_sem, sr_sem, as_sem, ar_sem, bs_sem, br_sem,
):
    half, hidden = WI.shape[2], WI.shape[1]
    R = X.shape[1] // 2
    U = R // 2
    bf16, f32 = jnp.bfloat16, jnp.float32
    n_exp = lax.axis_size("expert")
    me = lax.axis_index("expert")
    blk = lax.axis_index("blk")
    xl, z = blk // RING, blk % RING
    above = {"blk": xl * RING + (z + 1) % RING}
    below = {"blk": xl * RING + (z + RING - 1) % RING}
    pair = {"blk": (1 - xl) * RING + z}

    def remote(src, dst, ss, rs, peer):
        return pltpu.make_async_remote_copy(
            src_ref=src, dst_ref=dst, send_sem=ss, recv_sem=rs, device_id=peer, device_id_type=MESH
        )

    def expert_loop(body):
        lax.fori_loop(1, n_exp, lambda j, c: (body(j), c)[1], 0)

    def greet(j):
        peer = {"expert": (me + j) % n_exp}
        pl.semaphore_signal(barrier, inc=1, device_id=peer, device_id_type=MESH)

    barrier = pltpu.get_barrier_semaphore()
    expert_loop(greet)
    for peer in (above, below, pair):
        pl.semaphore_signal(barrier, inc=1, device_id=peer, device_id_type=MESH)

    T = send_ref.shape[0] // n_exp

    def piece(e):
        return pl.ds(pl.multiple_of(e * T, 16), T)

    mine = pl.ds(pl.multiple_of(xl * half, LANES), half)
    theirs = pl.ds(pl.multiple_of((1 - xl) * half, LANES), half)
    own_rows = pltpu.make_async_copy(send_ref.at[piece(me), :], GOT.at[piece(me), :], loc_sem.at[0])
    own_win = pltpu.make_async_copy(win_ref.at[:, mine], WI.at[xl], loc_sem.at[1])
    own_wdn = pltpu.make_async_copy(wdn_ref.at[:, mine], WD.at[xl], loc_sem.at[2])

    out_win = remote(win_ref.at[:, theirs], WI.at[xl], ws_sem.at[0], wr_sem.at[0], pair)
    out_wdn = remote(wdn_ref.at[:, theirs], WD.at[xl], ws_sem.at[1], wr_sem.at[1], pair)
    in_win = remote(win_ref.at[:, mine], WI.at[1 - xl], ws_sem.at[0], wr_sem.at[0], pair)
    in_wdn = remote(wdn_ref.at[:, mine], WD.at[1 - xl], ws_sem.at[1], wr_sem.at[1], pair)

    def to_expert(j):
        e = (me + j) % n_exp
        return remote(
            send_ref.at[piece(e), :], GOT.at[piece(me), :], as_sem.at[j], ar_sem.at[j], {"expert": e}
        )

    def to_token(j):
        e = (me + j) % n_exp
        return remote(TS.at[piece(e), :], out_ref.at[piece(me), :], bs_sem.at[j], br_sem.at[j], {"expert": e})

    own_rows.start()
    pl.semaphore_wait(barrier, n_exp - 1 + 3)
    expert_loop(lambda j: to_expert(j).start())
    out_win.start()
    own_win.start()
    own_wdn.start()

    size = CHUNKS * U
    slots = T // CHUNKS
    row = lax.broadcasted_iota(jnp.int32, (size, 1), 0)
    partner = ((row // slots) % CHUNKS) * U + (row // U) * slots + row % slots
    MIX[...] = (lax.broadcasted_iota(jnp.int32, (size, size), 1) == partner).astype(f32).astype(bf16)

    def at_below(u):
        return pl.ds(2 * U * u, U)

    def at_above(u):
        return pl.ds(U if u == 1 else 3 * U, U)

    def up(s, u):
        src = X.at[0, pl.ds(R + u * U, U), :] if s == 1 else X.at[s - 1, at_below(u), :]
        dst = X.at[s, at_below(u), :] if s < 4 else X.at[0, pl.ds(u * U, U), :]
        return remote(src, dst, us_sem.at[s - 1, u], ur_sem.at[s - 1, u], above)

    def down(s, u):
        src = X.at[0, pl.ds(R + u * U, U), :] if s == 1 else X.at[s - 1, at_above(u), :]
        dst = X.at[s, at_above(u), :] if s < 4 else X.at[0, pl.ds(u * U, U), :]
        return remote(src, dst, ds_sem.at[s - 1, u], dr_sem.at[s - 1, u], below)

    own_rows.wait()
    expert_loop(lambda j: to_expert(j).wait_recv())
    wide = GOT.shape[1]
    for u in range(2):
        TURN[...] = jnp.dot(
            MIX[...], GOT[u * size : u * size + size, :], preferred_element_type=f32
        ).astype(bf16)
        for k in range(CHUNKS):
            X[0, R + u * U : R + u * U + U, k * wide : (k + 1) * wide] = TURN[k * U : (k + 1) * U, :]
        if u == 0:
            up(1, 0).start()
    down(1, 1).start()
    up(1, 1).start()
    down(1, 0).start()
    own_win.wait()
    own_wdn.wait()

    def project(q, at, n, h, what):
        rows = pl.ds(at, n)
        if "p" in what:
            PRE[q, h, rows, :] = nt(X[q, rows, :half], WI[h])
        if "b" in what:
            BACK[q, h, rows, :] = nt(X[q, rows, half:], WD[h])

    project(0, R, R, xl, "pb")
    for s in range(1, 4):
        up(s, 0).wait_recv()
        up(s + 1, 0).start()
        down(s, 1).wait_recv()
        down(s + 1, 1).start()
        if s == 3:
            project(3, 0, R, xl, "pb")
        up(s, 1).wait_recv()
        if s < 3:
            up(s + 1, 1).start()
        down(s, 0).wait_recv()
        if s < 3:
            down(s + 1, 0).start()
            if s == 1:
                out_wdn.start()
            project(s, 0, 2 * R, xl, "pb")
        else:
            project(3, R, R, xl, "pb")
        if s == 2:
            in_win.wait_recv()
            project(1, 0, 2 * R, 1 - xl, "p")
            project(2, 0, 2 * R, 1 - xl, "p")
    project(3, 0, 2 * R, 1 - xl, "p")

    def swap(k):
        return remote(ES.at[k], ER.at[k], es_sem.at[k], er_sem.at[k], pair)

    def give(k):
        q, at = GROUPS[k][0], GROUPS[k][1] * R
        for h in range(2):
            ES[k, 0, h] = PRE[q, h, at : at + R, :].astype(bf16)
            ES[k, 1, h] = BACK[q, h, at : at + R, :].astype(bf16)
        swap(k).start()

    def terms(k):
        q, at = GROUPS[k][0], GROUPS[k][1] * R
        swap(k).wait_recv()
        gate = jnp.zeros((R, 1), f32)
        for h in range(2):
            pre = PRE[q, h, at : at + R, :] + ER[k, 0, h].astype(f32)
            back = BACK[q, h, at : at + R, :] + ER[k, 1, h].astype(f32)
            sigma = jax.nn.sigmoid(pre)
            act = pre * sigma
            gate = gate + jnp.sum(act * back, axis=1, keepdims=True)
            SL[h] = (back * sigma * (1.0 + pre * (1.0 - sigma))).astype(bf16)
        PART[:, half:] = jnp.broadcast_to(gate, (R, LANES))
        step = 4 * LANES

        def columns(c, carry):
            there = pl.ds(pl.multiple_of(c * step, step), step)
            PART[:, there] = jnp.dot(SL[0], WI[0, :, there], preferred_element_type=f32) + jnp.dot(
                SL[1], WI[1, :, there], preferred_element_type=f32
            )
            return carry

        lax.fori_loop(0, half // step, columns, 0)

    def pass_on(k, a):
        rows = pl.ds(a * U, U)
        peer = above if (a == 0) == (k == 1) else below
        return remote(SUM.at[k, rows, :], ARR.at[k, rows, :], ss_sem.at[k, a], sr_sem.at[k, a], peer)

    def arrived(k, a):
        pass_on(k, a).wait_recv()
        return ARR[k, a * U : a * U + U, :].astype(f32)

    def add_and_pass(k):
        terms(k)
        for a in range(2):
            term = PART[a * U : a * U + U, :]
            if BEFORE[k] is not None:
                b, crossed = BEFORE[k]
                term = term + arrived(b, 1 - a if crossed else a)
            SUM[k, a * U : a * U + U, :] = term.astype(bf16)
            pass_on(k, a).start()

    in_wdn.wait_recv()
    project(3, 0, 2 * R, 1 - xl, "b")
    give(0)
    project(2, 0, 2 * R, 1 - xl, "b")
    up(4, 0).wait_recv()
    down(4, 1).wait_recv()
    project(0, 0, R, xl, "pb")
    project(0, 0, 2 * R, 1 - xl, "pb")
    give(1)
    give(2)
    project(1, 0, 2 * R, 1 - xl, "b")
    add_and_pass(0)
    give(3)
    for k in range(1, 7):
        add_and_pass(k)
        if k + 3 < 8:
            give(k + 3)
    terms(7)

    def send_out(j):
        to_token(j).start()

    for a in range(2):
        total = (PART[a * U : a * U + U, :] + arrived(4, a) + arrived(6, 1 - a)).astype(bf16)
        third = half // CHUNKS
        for k in range(CHUNKS):
            TURN[k * U : (k + 1) * U, :third] = total[:, k * third : (k + 1) * third]
            TURN[k * U : (k + 1) * U, third : third + LANES] = total[:, half:]
        TS[a * size : a * size + size, :] = jnp.dot(
            MIX[...], TURN[:, : third + LANES], preferred_element_type=f32
        ).astype(bf16)
    expert_loop(send_out)
    own_back = pltpu.make_async_copy(TS.at[piece(me), :], out_ref.at[piece(me), :], loc_sem.at[3])
    own_back.start()

    out_win.wait_send()
    out_wdn.wait_send()
    expert_loop(lambda j: to_expert(j).wait_send())
    for s in range(1, 5):
        for u in range(2):
            if s < 4 or u == 0:
                up(s, u).wait_send()
            if s < 4 or u == 1:
                down(s, u).wait_send()
    for k in range(8):
        swap(k).wait_send()
    for k in range(7):
        for a in range(2):
            pass_on(k, a).wait_send()
    own_back.wait()
    expert_loop(lambda j: to_token(j).wait())


def expert_rows(send, w_in, w_down, slots):
    n_exp = lax.axis_size("expert")
    hidden, width = w_in.shape
    half = width // 2
    n_rows = n_exp * slots
    wide = half + LANES
    back = half // CHUNKS + LANES
    bf16, f32, dma = jnp.bfloat16, jnp.float32, pltpu.SemaphoreType.DMA
    return pl.pallas_call(
        kernel,
        out_shape=jax.ShapeDtypeStruct((send.shape[0], back), bf16),
        in_specs=[pl.BlockSpec(memory_space=pl.ANY)] * 3,
        out_specs=pl.BlockSpec(memory_space=pltpu.VMEM),
        scratch_shapes=[
            pltpu.VMEM(send.shape, bf16),
            pltpu.VMEM((4, 2 * n_rows, width), bf16),
            pltpu.VMEM((2, hidden, half), bf16),
            pltpu.VMEM((2, hidden, half), bf16),
            pltpu.VMEM((4, 2, 2 * n_rows, hidden), f32),
            pltpu.VMEM((4, 2, 2 * n_rows, hidden), f32),
            pltpu.VMEM((8, 2, 2, n_rows, hidden), bf16),
            pltpu.VMEM((8, 2, 2, n_rows, hidden), bf16),
            pltpu.VMEM((2, n_rows, hidden), bf16),
            pltpu.VMEM((n_rows, wide), f32),
            pltpu.VMEM((7, n_rows, wide), bf16),
            pltpu.VMEM((7, n_rows, wide), bf16),
            pltpu.VMEM((send.shape[0] // 2, send.shape[0] // 2), bf16),
            pltpu.VMEM((send.shape[0] // 2, send.shape[1]), bf16),
            pltpu.VMEM((send.shape[0], back), bf16),
            dma((4,)), dma((2,)), dma((2,)),
            dma((4, 2)), dma((4, 2)), dma((4, 2)), dma((4, 2)),
            dma((8,)), dma((8,)),
            dma((7, 2)), dma((7, 2)),
            dma((n_exp,)), dma((n_exp,)), dma((n_exp,)), dma((n_exp,)),
        ],
        compiler_params=pltpu.CompilerParams(
            collective_id=0, has_side_effects=True, vmem_limit_bytes=60 * 2**20
        ),
    )(send, w_in, w_down)


def per_device(tokens, out_grad, expert_ids, slots, gates, w_in, w_down):
    tok_count, width = tokens.shape
    half = width // 2
    top_count = expert_ids.shape[1]
    expert_count, blk_count = lax.axis_size("expert"), lax.axis_size("blk")
    capacity = max(2, (tok_count * top_count + expert_count - 1) // expert_count + 1)
    swap = [(i, (i + RING) % blk_count) for i in range(blk_count)]
    xl = lax.axis_index("blk") // RING

    def cut(a, side):
        return lax.dynamic_slice(a, (0, side * half), (tok_count, half))

    small = jnp.concatenate(
        [(expert_ids * (2 * capacity) + slots + capacity * xl).astype(jnp.bfloat16), gates], axis=1
    )
    small = jnp.pad(small, ((0, 0), (0, LANES - 2 * top_count)))
    away = jnp.concatenate([cut(tokens, 1 - xl), cut(out_grad, 1 - xl), small], axis=1)
    stay = jnp.concatenate([cut(tokens, xl), cut(out_grad, xl), small], axis=1)
    came = lax.ppermute(away, "blk", swap)
    both = jnp.concatenate([stay, came], axis=0)
    target = both[:, width : width + top_count].astype(jnp.int32)
    weight = both[:, width + top_count : width + 2 * top_count].astype(jnp.float32)
    slot_count = 2 * capacity
    n_tok = 2 * tok_count
    row = jnp.arange(expert_count * CHUNKS * slot_count, dtype=jnp.int32)
    row_target = row // (CHUNKS * slot_count) * slot_count + row % slot_count
    row_piece = row // slot_count % CHUNKS
    matches = (target[None] == row_target[:, None, None]).astype(jnp.float32)
    placing = jnp.sum(matches, axis=2)
    weighed = jnp.sum(matches * weight[None], axis=2)
    same = (row_piece[:, None] == jnp.arange(CHUNKS)[None]).astype(jnp.float32)

    def pieces(a):
        return (same[:, :, None] * a[:, None, :]).reshape(row.shape[0], CHUNKS * n_tok).astype(jnp.bfloat16)

    piece = width // CHUNKS
    stacked = jnp.concatenate([both[:, k * piece : (k + 1) * piece] for k in range(CHUNKS)], axis=0)
    send = jnp.dot(pieces(placing), stacked, preferred_element_type=jnp.float32).astype(jnp.bfloat16)
    back = expert_rows(send, w_in[0], w_down[0], slot_count)
    part = half // CHUNKS
    grad = lax.dot_general(
        pieces(weighed), back[:, :part], (((0,), (0,)), ((), ())), preferred_element_type=jnp.float32
    ).astype(jnp.bfloat16)
    grad = jnp.concatenate([grad[k * n_tok : (k + 1) * n_tok] for k in range(CHUNKS)], axis=1)
    own, other = grad[:tok_count], grad[tok_count:]
    other = lax.ppermute(other, "blk", swap)
    grad_tokens = jnp.where(
        xl == 0, jnp.concatenate([own, other], axis=1), jnp.concatenate([other, own], axis=1)
    )
    first = (row_piece == 0).astype(jnp.float32) * back[:, part].astype(jnp.float32)
    grad_gates = jnp.einsum("stk,s->tk", matches[:, :tok_count], first).astype(jnp.bfloat16)
    return (grad_tokens, grad_gates)


def solution(mesh):
    return jax.shard_map(
        per_device,
        mesh=mesh,
        in_specs=(
            P(("expert", "blk"), None),
            P(("expert", "blk"), None),
            P(("expert", "blk"), None),
            P(("expert", "blk"), None),
            P(("expert", "blk"), None),
            P("expert", "blk", None),
            P("expert", "blk", None),
        ),
        out_specs=(P(("expert", "blk"), None), P(("expert", "blk"), None)),
        check_vma=False,
    )
```

time: 418 us -> 207 us (0.50)
  Pallas kernels: 0 us -> 190 us
  waiting for transfers between devices: 142 us -> 2.81 us
  starting transfers between devices: 118 us -> 3.5 us
  blocking collectives: 100 us -> 0 us
  matrix products: 32 us -> 3.03 us
  between operations: 15.1 us -> 0.83 us
  local copies, waits for them, and re-layouts: 8.4 us -> 3.43 us
    pallas_call x0 -> x1, Pallas kernels: none -> 190 us  [expert_rows(): pl.pallas_call(kernel, out_shape=jax.ShapeDtypeStruct((send.shape[0], bac...]
    all_to_all x3 -> x0, starting transfers between devices: 118 us -> none  [the longest x1 99 us: per_device(): lax.all_to_all(send_gate, 'expert', split_axis=0, concat_axis=0, tiled=True)]
    reduce_scatter x1 -> x0, waiting for transfers between devices: 68.8 us -> none  [per_device(): lax.psum_scatter(jnp.dot(slope, weight_in, preferred_element_type=jnp.flo...]
    unnamed x2 -> x0, blocking collectives: 60.1 us -> none
    all_gather x2 -> x0, waiting for transfers between devices: 53.6 us -> none  [the longest x1 53.5 us: per_device(): lax.all_gather(recv_dy, 'blk', axis=0, tiled=True)]
    all_to_all x2 -> x0, blocking collectives: 40.3 us -> none  [the longest x1 22.5 us: per_device(): lax.all_to_all(send_x, 'expert', split_axis=0, concat_axis=0, tiled=True)]
    dot_general x8 -> x3, matrix products: 32 us -> 3.03 us  [the longest x1 1.5 us: per_device(): jnp.dot(pieces(placing), stacked, preferred_element_type=jnp.float32)]
    all_to_all x3 -> x0, waiting for transfers between devices: 19.2 us -> none  [the longest x1 13.5 us: per_device(): lax.all_to_all(grad_rows, 'expert', split_axis=0, concat_axis=0, tiled=True)]
  transfers between devices with their start and end apart: 6 -> 2, of which waited for: 4 -> 2; matrix products, arithmetic and copies ran while one was open for 3% -> 0% of each run, Pallas kernels for 0% -> 0%
where the time goes in v2:
time: 207 us; the launch traced here: 206 us
  Pallas kernels  190 us (92%)
  starting transfers between devices  3.5 us (2%)
  local copies, waits for them, and re-layouts  3.43 us (2%)
  matrix products  3.03 us (1%)
  other arithmetic  2.86 us (1%)
  waiting for transfers between devices  2.81 us (1%)
    pallas_call x1, Pallas kernels, expert_rows(): pl.pallas_call(kernel, out_shape=jax.ShapeDtypeStruct((send.shape[0], bac...  190 us
  transfers between devices with their start and end apart: 2, of which 2 were waited for; matrix products, arithmetic and copies ran while one was open for 0% of the time, Pallas kernels for 0%

profile of v2, /device:TPU:1, one launch (start us, length us, event | category | flops | bytes accessed | tf_op | source)
XLA Modules:
  0.0 206.2 jit_solution(4603369349314453362)
XLA Ops:
  0.7 0.8 copy.23
  1.4 0.8 copy.22
  2.2 0.8 copy.21
  2.9 0.1 fusion.18
  3.0 0.9 constant_dynamic-slice_fusion.2
  3.9 2.1 %collective-permute-start = (bf16[8,6272]{1,0:T(8,128)(2,1)S(1)}, bf16[8,6272]{1,0:T(8,128)(2,1)S(1)}, u32[]{:S(2)}, u32[]{:S(2)}) collective-permute-start(bf16[8,6272]{1,0:T(8,128)(2,1)S(1)} %pad_maximum_fusion), channel_id=1, source_target_pairs={{0,8},{1,9},{2,10},{3,11},{4,12},{5,13},{6,14},{7,15},{8,0},{9,1},... | collective-permute-start | bytes 301064 | tf_op jit(solution)/shard_map/ppermute | solution.py:327
  6.1 2.0 collective-permute-done
  8.1 0.1 pad_maximum_fusion.4
  8.2 0.1 copy.27
  8.3 0.1 copy.28
  8.4 0.1 broadcast_compare_fusion
  8.5 0.1 convert_reduce_fusion.1
  8.7 1.5 convolution_convert_fusion.send_ref
  10.2 189.7 %shard_map.86 = bf16[768,512]{1,0:T(8,128)(2,1)} custom-call(bf16[768,768]{1,0:T(8,128)(2,1)} %convolution_convert_fusion.send_ref, bf16[336,6144]{1,0:T(8,128)(2,1)} %bitcast.11, bf16[336,6144]{1,0:T(8,128)(2,1)} %bitcast.12), custom_call_target="tpu_custom_call" | custom-call | tf_op jit(solution)/shard_map/pallas_call | solution.py:276
  200.0 1.1 convert_reduce_fusion
  201.0 1.3 convolution_convert_fusion.1
  202.5 1.4 collective-permute-start.1
  203.9 0.2 fusion.1
  204.1 0.6 convert_element_type.64
  204.7 0.8 collective-permute-done.1
  205.5 0.7 maximum_select_fusion
  (27 shorter events, 0.3 us)
Async XLA Ops:
  3.9 4.2 %collective-permute-start = (bf16[8,6272]{1,0:T(8,128)(2,1)S(1)}, bf16[8,6272]{1,0:T(8,128)(2,1)S(1)}, u32[]{:S(2)}, u32[]{:S(2)}) collective-permute-start(bf16[8,6272]{1,0:T(8,128)(2,1)S(1)} %pad_maximum_fusion), channel_id=1, source_target_pairs={{0,8},{1,9},{2,10},{3,11},{4,12},{5,13},{6,14},{7,15},{8,0},{9,1},... | collective-permute-start | bytes 301064 | tf_op jit(solution)/shard_map/ppermute | solution.py:327
  202.5 3.0 %collective-permute-start.1 = (bf16[8,3072]{1,0:T(8,128)(2,1)S(1)}, bf16[8,3072]{1,0:T(8,128)(2,1)S(1)}, u32[]{:S(2)}, u32[]{:S(2)}) collective-permute-start(bf16[8,3072]{1,0:T(8,128)(2,1)S(1)} %get-tuple-element.7), channel_id=1, source_target_pairs={{0,8},{1,9},{2,10},{3,11},{4,12},{5,13},{6,14},{7,15},{8,0},{9,1},... | collective-permute-start | bytes 147464 | tf_op jit(solution)/shard_map/ppermute | solution.py:354

commit v3 on v2

--- a/solution.py
+++ b/solution.py
@@ -22,10 +22,10 @@
 
 
 def kernel(
-    send_ref, win_ref, wdn_ref, out_ref,
-    GOT, X, WI, WD, PRE, BACK, ES, ER, SL, PART, SUM, ARR, MIX, TURN, TS,
+    raw_ref, far_ref, win_ref, wdn_ref, out_ref,
+    RAW, OUT, GOT, FAR, X, WI, WD, PRE, BACK, ES, ER, SL, PART, SUM, ARR, MIX, TURN, TS,
     loc_sem, ws_sem, wr_sem, us_sem, ur_sem, ds_sem, dr_sem, es_sem, er_sem,
-    ss_sem, sr_sem, as_sem, ar_sem, bs_sem, br_sem,
+    ss_sem, sr_sem, as_sem, ar_sem, bs_sem, br_sem, ts_sem, tr_sem, ys_sem, yr_sem,
 ):
     half, hidden = WI.shape[2], WI.shape[1]
     R = X.shape[1] // 2
@@ -33,6 +33,8 @@
     bf16, f32 = jnp.bfloat16, jnp.float32
     n_exp = lax.axis_size("expert")
     me = lax.axis_index("expert")
+    near = n_exp // 2
+    side, seat = me // near, me % near
     blk = lax.axis_index("blk")
     xl, z = blk // RING, blk % RING
     above = {"blk": xl * RING + (z + 1) % RING}
@@ -56,14 +58,23 @@
     for peer in (above, below, pair):
         pl.semaphore_signal(barrier, inc=1, device_id=peer, device_id_type=MESH)
 
-    T = send_ref.shape[0] // n_exp
+    def across(j):
+        return {"expert": (1 - side) * near + (seat + j) % near, "blk": (1 - xl) * RING + z}
+
+    def greet_across(j, carry):
+        pl.semaphore_signal(barrier, inc=1, device_id=across(j), device_id_type=MESH)
+        return carry
+
+    lax.fori_loop(0, near, greet_across, 0)
+
+    T = far_ref.shape[0] // near
 
     def piece(e):
         return pl.ds(pl.multiple_of(e * T, 16), T)
 
     mine = pl.ds(pl.multiple_of(xl * half, LANES), half)
     theirs = pl.ds(pl.multiple_of((1 - xl) * half, LANES), half)
-    own_rows = pltpu.make_async_copy(send_ref.at[piece(me), :], GOT.at[piece(me), :], loc_sem.at[0])
+    own_raw = pltpu.make_async_copy(raw_ref, RAW.at[0], loc_sem.at[0])
     own_win = pltpu.make_async_copy(win_ref.at[:, mine], WI.at[xl], loc_sem.at[1])
     own_wdn = pltpu.make_async_copy(wdn_ref.at[:, mine], WD.at[xl], loc_sem.at[2])
 
@@ -72,19 +83,59 @@
     in_win = remote(win_ref.at[:, mine], WI.at[1 - xl], ws_sem.at[0], wr_sem.at[0], pair)
     in_wdn = remote(wdn_ref.at[:, mine], WD.at[1 - xl], ws_sem.at[1], wr_sem.at[1], pair)
 
-    def to_expert(j):
-        e = (me + j) % n_exp
+    def to_far(j):
+        e = (seat + j) % near
+        return remote(far_ref.at[piece(e), :], FAR.at[piece(seat), :], as_sem.at[j], ar_sem.at[j], across(j))
+
+    def to_near(r, j):
+        e = (seat + j) % near
         return remote(
-            send_ref.at[piece(e), :], GOT.at[piece(me), :], as_sem.at[j], ar_sem.at[j], {"expert": e}
+            OUT.at[r, piece(e), :], GOT.at[r, piece(seat), :], ys_sem.at[r, j], yr_sem.at[r, j],
+            {"expert": side * near + e},
         )
+
+    def near_own(r):
+        return pltpu.make_async_copy(OUT.at[r, piece(seat), :], GOT.at[r, piece(seat), :], ys_sem.at[r, 0])
+
+    def near_loop(r, body):
+        lax.fori_loop(1, near, lambda j, c: (body(to_near(r, j)), c)[1], 0)
+
+    def far_loop(body):
+        lax.fori_loop(0, near, lambda j, c: (body(to_far(j)), c)[1], 0)
 
     def to_token(j):
         e = (me + j) % n_exp
-        return remote(TS.at[piece(e), :], out_ref.at[piece(me), :], bs_sem.at[j], br_sem.at[j], {"expert": e})
-
-    own_rows.start()
-    pl.semaphore_wait(barrier, n_exp - 1 + 3)
-    expert_loop(lambda j: to_expert(j).start())
+        a = (e // near + side) % 2
+        return remote(
+            TS.at[piece(a * near + e % near), :], out_ref.at[piece(me), :], bs_sem.at[j], br_sem.at[j],
+            {"expert": e},
+        )
+
+    def raw_rows(a):
+        return pl.ds(0, 80) if a == 0 else pl.ds(80, RAW.shape[1] - 80)
+
+    def raw_up(s, a):
+        return remote(
+            RAW.at[s - 1, raw_rows(a), :], RAW.at[s, raw_rows(a), :], ts_sem.at[0, s - 1, a],
+            tr_sem.at[0, s - 1, a], above,
+        )
+
+    def raw_down(s, a):
+        src = 0 if s == 1 else RING // 2 + s - 1
+        dst = RING // 2 + s if s < 4 else 4
+        return remote(
+            RAW.at[src, raw_rows(a), :], RAW.at[dst, raw_rows(a), :], ts_sem.at[1, s - 1, a],
+            tr_sem.at[1, s - 1, a], below,
+        )
+
+    own_raw.start()
+    own_raw.wait()
+    pl.semaphore_wait(barrier, n_exp - 1 + 3 + near)
+    raw_up(1, 0).start()
+    raw_down(1, 1).start()
+    raw_up(1, 1).start()
+    raw_down(1, 0).start()
+    far_loop(lambda c: c.start())
     out_win.start()
     own_win.start()
     own_wdn.start()
@@ -95,38 +146,73 @@
     partner = ((row // slots) % CHUNKS) * U + (row // U) * slots + row % slots
     MIX[...] = (lax.broadcasted_iota(jnp.int32, (size, size), 1) == partner).astype(f32).astype(bf16)
 
-    def at_below(u):
-        return pl.ds(2 * U * u, U)
-
-    def at_above(u):
-        return pl.ds(U if u == 1 else 3 * U, U)
-
-    def up(s, u):
-        src = X.at[0, pl.ds(R + u * U, U), :] if s == 1 else X.at[s - 1, at_below(u), :]
-        dst = X.at[s, at_below(u), :] if s < 4 else X.at[0, pl.ds(u * U, U), :]
-        return remote(src, dst, us_sem.at[s - 1, u], ur_sem.at[s - 1, u], above)
-
-    def down(s, u):
-        src = X.at[0, pl.ds(R + u * U, U), :] if s == 1 else X.at[s - 1, at_above(u), :]
-        dst = X.at[s, at_above(u), :] if s < 4 else X.at[0, pl.ds(u * U, U), :]
-        return remote(src, dst, ds_sem.at[s - 1, u], dr_sem.at[s - 1, u], below)
-
-    own_rows.wait()
-    expert_loop(lambda j: to_expert(j).wait_recv())
-    wide = GOT.shape[1]
-    for u in range(2):
-        TURN[...] = jnp.dot(
-            MIX[...], GOT[u * size : u * size + size, :], preferred_element_type=f32
-        ).astype(bf16)
+    tok = (RAW.shape[1] - 16) // CHUNKS
+    wanted = ((side * near + row // T) * slots + row % slots).astype(f32)
+    piece_of = (row // slots) % CHUNKS
+    lane = lax.broadcasted_iota(jnp.int32, (1, CHUNKS * tok), 1) // tok
+
+    def place(r):
+        table = RAW[r, CHUNKS * tok : CHUNKS * tok + 16, : CHUNKS * tok].astype(f32)
+        hit = jnp.zeros((size, CHUNKS * tok), f32)
+        for k in range(4):
+            hit = hit + (table[k : k + 1, :] == wanted).astype(f32)
+        hit = jnp.where(piece_of == lane, hit, 0.0).astype(bf16)
+        OUT[r] = jnp.dot(hit, RAW[r, : CHUNKS * tok, :], preferred_element_type=f32).astype(bf16)
+        near_loop(r, lambda c: c.start())
+        near_own(r).start()
+
+    wide = FAR.shape[1]
+
+    def turned(got, q, at):
+        TURN[...] = jnp.dot(MIX[...], got, preferred_element_type=f32).astype(bf16)
         for k in range(CHUNKS):
-            X[0, R + u * U : R + u * U + U, k * wide : (k + 1) * wide] = TURN[k * U : (k + 1) * U, :]
-        if u == 0:
+            X[q, at : at + U, k * wide : (k + 1) * wide] = TURN[k * U : (k + 1) * U, :]
+
+    def settle(r, q, at):
+        near_own(r).wait()
+        near_loop(r, lambda c: c.wait_recv())
+        turned(GOT[r], q, at)
+
+    def cols(a):
+        return pl.ds(a * half, half)
+
+    def up(s, a):
+        src = X.at[0, pl.ds(3 * U, U), cols(a)] if s == 1 else X.at[s - 1, pl.ds(2 * U, U), cols(a)]
+        dst = X.at[s, pl.ds(2 * U, U), cols(a)] if s < 4 else X.at[0, pl.ds(U, U), cols(a)]
+        return remote(src, dst, us_sem.at[s - 1, a], ur_sem.at[s - 1, a], above)
+
+    def down(s, a):
+        src = X.at[0, pl.ds(3 * U, U), cols(a)] if s == 1 else X.at[s - 1, pl.ds(U, U), cols(a)]
+        dst = X.at[s % 4, pl.ds(U, U), cols(a)]
+        return remote(src, dst, ds_sem.at[s - 1, a], dr_sem.at[s - 1, a], below)
+
+    place(0)
+    for s in range(1, 4):
+        raw_up(s, 0).wait_recv()
+        raw_up(s + 1, 0).start()
+        raw_down(s, 1).wait_recv()
+        raw_down(s + 1, 1).start()
+        raw_up(s, 1).wait_recv()
+        if s < 3:
+            raw_up(s + 1, 1).start()
+        raw_down(s, 0).wait_recv()
+        if s < 3:
+            raw_down(s + 1, 0).start()
+        else:
+            far_loop(lambda c: c.wait_recv())
+            turned(FAR[...], 0, 3 * U)
             up(1, 0).start()
-    down(1, 1).start()
-    up(1, 1).start()
-    down(1, 0).start()
+            down(1, 1).start()
+            up(1, 1).start()
+            down(1, 0).start()
+        place(s)
+        place(RING // 2 + s)
+    raw_up(4, 0).wait_recv()
+    raw_down(4, 1).wait_recv()
+    place(4)
     own_win.wait()
     own_wdn.wait()
+    settle(0, 0, 2 * U)
 
     def project(q, at, n, h, what):
         rows = pl.ds(at, n)
@@ -141,24 +227,24 @@
         up(s + 1, 0).start()
         down(s, 1).wait_recv()
         down(s + 1, 1).start()
-        if s == 3:
-            project(3, 0, R, xl, "pb")
         up(s, 1).wait_recv()
         if s < 3:
             up(s + 1, 1).start()
         down(s, 0).wait_recv()
         if s < 3:
             down(s + 1, 0).start()
-            if s == 1:
-                out_wdn.start()
-            project(s, 0, 2 * R, xl, "pb")
-        else:
-            project(3, R, R, xl, "pb")
-        if s == 2:
-            in_win.wait_recv()
-            project(1, 0, 2 * R, 1 - xl, "p")
-            project(2, 0, 2 * R, 1 - xl, "p")
-    project(3, 0, 2 * R, 1 - xl, "p")
+        if s == 1:
+            out_wdn.start()
+        settle(s, s, 0)
+        settle(RING // 2 + s, s, 3 * U)
+        project(s, 0, 2 * R, xl, "pb")
+    up(4, 0).wait_recv()
+    down(4, 1).wait_recv()
+    settle(4, 0, 0)
+    project(0, 0, R, xl, "pb")
+    in_win.wait_recv()
+    for q in range(4):
+        project(q, 0, 2 * R, 1 - xl, "p")
 
     def swap(k):
         return remote(ES.at[k], ER.at[k], es_sem.at[k], er_sem.at[k], pair)
@@ -215,12 +301,9 @@
     in_wdn.wait_recv()
     project(3, 0, 2 * R, 1 - xl, "b")
     give(0)
+    project(0, 0, 2 * R, 1 - xl, "b")
+    give(1)
     project(2, 0, 2 * R, 1 - xl, "b")
-    up(4, 0).wait_recv()
-    down(4, 1).wait_recv()
-    project(0, 0, R, xl, "pb")
-    project(0, 0, 2 * R, 1 - xl, "pb")
-    give(1)
     give(2)
     project(1, 0, 2 * R, 1 - xl, "b")
     add_and_pass(0)
@@ -244,12 +327,20 @@
             MIX[...], TURN[:, : third + LANES], preferred_element_type=f32
         ).astype(bf16)
     expert_loop(send_out)
-    own_back = pltpu.make_async_copy(TS.at[piece(me), :], out_ref.at[piece(me), :], loc_sem.at[3])
+    own_back = pltpu.make_async_copy(TS.at[piece(seat), :], out_ref.at[piece(me), :], loc_sem.at[3])
     own_back.start()
 
     out_win.wait_send()
     out_wdn.wait_send()
-    expert_loop(lambda j: to_expert(j).wait_send())
+    far_loop(lambda c: c.wait_send())
+    for r in range(RING):
+        near_loop(r, lambda c: c.wait_send())
+    for s in range(1, 5):
+        for a in range(2):
+            if s < 4 or a == 0:
+                raw_up(s, a).wait_send()
+            if s < 4 or a == 1:
+                raw_down(s, a).wait_send()
     for s in range(1, 5):
         for u in range(2):
             if s < 4 or u == 0:
@@ -265,7 +356,7 @@
     expert_loop(lambda j: to_token(j).wait())
 
 
-def expert_rows(send, w_in, w_down, slots):
+def expert_rows(raw, far, w_in, w_down, slots):
     n_exp = lax.axis_size("expert")
     hidden, width = w_in.shape
     half = width // 2
@@ -275,11 +366,14 @@
     bf16, f32, dma = jnp.bfloat16, jnp.float32, pltpu.SemaphoreType.DMA
     return pl.pallas_call(
         kernel,
-        out_shape=jax.ShapeDtypeStruct((send.shape[0], back), bf16),
-        in_specs=[pl.BlockSpec(memory_space=pl.ANY)] * 3,
+        out_shape=jax.ShapeDtypeStruct((2 * far.shape[0], back), bf16),
+        in_specs=[pl.BlockSpec(memory_space=pl.ANY)] * 4,
         out_specs=pl.BlockSpec(memory_space=pltpu.VMEM),
         scratch_shapes=[
-            pltpu.VMEM(send.shape, bf16),
+            pltpu.VMEM((RING,) + raw.shape, bf16),
+            pltpu.VMEM((RING,) + far.shape, bf16),
+            pltpu.VMEM((RING,) + far.shape, bf16),
+            pltpu.VMEM(far.shape, bf16),
             pltpu.VMEM((4, 2 * n_rows, width), bf16),
             pltpu.VMEM((2, hidden, half), bf16),
             pltpu.VMEM((2, hidden, half), bf16),
@@ -291,19 +385,20 @@
             pltpu.VMEM((n_rows, wide), f32),
             pltpu.VMEM((7, n_rows, wide), bf16),
             pltpu.VMEM((7, n_rows, wide), bf16),
-            pltpu.VMEM((send.shape[0] // 2, send.shape[0] // 2), bf16),
-            pltpu.VMEM((send.shape[0] // 2, send.shape[1]), bf16),
-            pltpu.VMEM((send.shape[0], back), bf16),
+            pltpu.VMEM((far.shape[0], far.shape[0]), bf16),
+            pltpu.VMEM(far.shape, bf16),
+            pltpu.VMEM((2 * far.shape[0], back), bf16),
             dma((4,)), dma((2,)), dma((2,)),
             dma((4, 2)), dma((4, 2)), dma((4, 2)), dma((4, 2)),
             dma((8,)), dma((8,)),
             dma((7, 2)), dma((7, 2)),
-            dma((n_exp,)), dma((n_exp,)), dma((n_exp,)), dma((n_exp,)),
+            dma((n_exp // 2,)), dma((n_exp // 2,)), dma((n_exp,)), dma((n_exp,)),
+            dma((2, 4, 2)), dma((2, 4, 2)), dma((RING, n_exp // 2)), dma((RING, n_exp // 2)),
         ],
         compiler_params=pltpu.CompilerParams(
             collective_id=0, has_side_effects=True, vmem_limit_bytes=60 * 2**20
         ),
-    )(send, w_in, w_down)
+    )(raw, far, w_in, w_down)
 
 
 def per_device(tokens, out_grad, expert_ids, slots, gates, w_in, w_down):
@@ -315,19 +410,18 @@
     swap = [(i, (i + RING) % blk_count) for i in range(blk_count)]
     xl = lax.axis_index("blk") // RING
 
-    def cut(a, side):
-        return lax.dynamic_slice(a, (0, side * half), (tok_count, half))
+    def cut(a, at, side):
+        return lax.dynamic_slice(a, (0, at * width + side * half), (tok_count, half))
 
     small = jnp.concatenate(
         [(expert_ids * (2 * capacity) + slots + capacity * xl).astype(jnp.bfloat16), gates], axis=1
     )
     small = jnp.pad(small, ((0, 0), (0, LANES - 2 * top_count)))
-    away = jnp.concatenate([cut(tokens, 1 - xl), cut(out_grad, 1 - xl), small], axis=1)
-    stay = jnp.concatenate([cut(tokens, xl), cut(out_grad, xl), small], axis=1)
+    away = jnp.concatenate([tokens, out_grad, small], axis=1)
     came = lax.ppermute(away, "blk", swap)
-    both = jnp.concatenate([stay, came], axis=0)
-    target = both[:, width : width + top_count].astype(jnp.int32)
-    weight = both[:, width + top_count : width + 2 * top_count].astype(jnp.float32)
+    small = jnp.concatenate([small, came[:, 2 * width :]], axis=0)
+    target = small[:, :top_count].astype(jnp.int32)
+    weight = small[:, top_count : 2 * top_count].astype(jnp.float32)
     slot_count = 2 * capacity
     n_tok = 2 * tok_count
     row = jnp.arange(expert_count * CHUNKS * slot_count, dtype=jnp.int32)
@@ -341,10 +435,24 @@
     def pieces(a):
         return (same[:, :, None] * a[:, None, :]).reshape(row.shape[0], CHUNKS * n_tok).astype(jnp.bfloat16)
 
-    piece = width // CHUNKS
-    stacked = jnp.concatenate([both[:, k * piece : (k + 1) * piece] for k in range(CHUNKS)], axis=0)
-    send = jnp.dot(pieces(placing), stacked, preferred_element_type=jnp.float32).astype(jnp.bfloat16)
-    back = expert_rows(send, w_in[0], w_down[0], slot_count)
+    def stacked(side):
+        rows = [
+            jnp.concatenate([cut(a, 0, side), cut(b, at, side)], axis=1)
+            for a, b, at in ((tokens, out_grad, 0), (came, came, 1))
+        ]
+        both = jnp.concatenate(rows, axis=0)
+        piece = width // CHUNKS
+        return jnp.concatenate([both[:, k * piece : (k + 1) * piece] for k in range(CHUNKS)], axis=0)
+
+    near = row.shape[0] // 2
+    x_hi = lax.axis_index("expert") // (expert_count // 2)
+    raw = stacked(xl)
+    table = jnp.tile(small[:, :top_count].T, (1, CHUNKS))
+    table = jnp.pad(table, ((0, 16 - top_count), (0, raw.shape[1] - table.shape[1])), constant_values=-1)
+    raw = jnp.concatenate([raw, table], axis=0)
+    far = lax.dynamic_slice(pieces(placing), ((1 - x_hi) * near, 0), (near, CHUNKS * n_tok))
+    far = jnp.dot(far, stacked(1 - xl), preferred_element_type=jnp.float32).astype(jnp.bfloat16)
+    back = expert_rows(raw, far, w_in[0], w_down[0], slot_count)
     part = half // CHUNKS
     grad = lax.dot_general(
         pieces(weighed), back[:, :part], (((0,), (0,)), ((), ())), preferred_element_type=jnp.float32

time: 207 us -> 193 us (0.932)
  Pallas kernels: 190 us -> 173 us
    pallas_call x1, Pallas kernels: 190 us -> 173 us  [expert_rows(): pl.pallas_call(kernel, out_shape=jax.ShapeDtypeStruct((2 * far.shape[0],...]
  transfers between devices with their start and end apart: 2 -> 2, of which waited for: 2 -> 2; matrix products, arithmetic and copies ran while one was open for 0% -> 1% of each run, Pallas kernels for 0% -> 0%
where the time goes in v3:
time: 193 us; the launch traced here: 191 us
  Pallas kernels  173 us (90%)
  local copies, waits for them, and re-layouts  4.48 us (2%)
  starting transfers between devices  3.96 us (2%)
  other arithmetic  3.77 us (2%)
  matrix products  2.69 us (1%)
  waiting for transfers between devices  2.27 us (1%)
    pallas_call x1, Pallas kernels, expert_rows(): pl.pallas_call(kernel, out_shape=jax.ShapeDtypeStruct((2 * far.shape[0],...  173 us
  transfers between devices with their start and end apart: 2, of which 2 were waited for; matrix products, arithmetic and copies ran while one was open for 1% of the time, Pallas kernels for 0%

profile of v3, /device:TPU:1, one launch (start us, length us, event | category | flops | bytes accessed | tf_op | source)
XLA Modules:
  0.0 191.2 jit_solution(13240096486531077706)
XLA Ops:
  0.6 0.8 copy.25
  1.4 0.8 copy.24
  2.2 0.8 copy.23
  2.9 0.1 fusion.21
  3.0 1.0 pad_maximum_fusion
  4.0 2.1 %collective-permute-start = (bf16[8,12416]{1,0:T(8,128)(2,1)S(1)}, bf16[8,12416]{1,0:T(8,128)(2,1)S(1)}, u32[]{:S(2)}, u32[]{:S(2)}) collective-permute-start(bf16[8,12416]{1,0:T(8,128)(2,1)S(1)} %pad_maximum_fusion), channel_id=1, source_target_pairs={{0,8},{1,9},{2,10},{3,11},{4,12},{5,13},{6,14},{7,15},{8,0},{9,1},... | collective-permute-start | bytes 595976 | tf_op jit(solution)/shard_map/ppermute | solution.py:421
  6.1 0.8 constant_dynamic-slice_fusion.2
  7.0 0.8 constant_dynamic-slice_fusion.3
  7.8 1.6 collective-permute-done
  9.4 0.1 fusion.22
  9.5 0.1 copy.26
  9.6 0.1 copy.27
  9.7 0.1 broadcast_compare_fusion
  9.8 0.1 convert_reduce_fusion.1
  10.0 0.1 copy.28
  10.1 0.1 tile.10
  10.3 0.0 copy-start
  10.4 1.2 convolution_convert_fusion.far_ref
  11.6 0.0 copy-done
  11.6 173.2 %shard_map.86 = bf16[768,512]{1,0:T(8,128)(2,1)} custom-call(bf16[144,768]{1,0:T(8,128)(2,1)} %copy-done, bf16[384,768]{1,0:T(8,128)(2,1)} %convolution_convert_fusion.far_ref, bf16[336,6144]{1,0:T(8,128)(2,1)} %bitcast.12, bf16[336,6144]{1,0:T(8,128)(2,1)} %bitcast.13), custom_call_target="tpu_custom_call" | custom-call | tf_op jit(solution)/shard_map/pallas_call | solution.py:367
  184.7 1.1 convert_reduce_fusion
  185.8 1.3 convolution_convert_fusion.1
  187.3 1.8 collective-permute-start.1
  189.1 0.2 fusion.2
  189.3 0.6 convert_element_type.66
  189.9 0.7 collective-permute-done.1
  190.6 0.7 maximum_select_fusion
  (36 shorter events, 0.3 us)
Async XLA Ops:
  4.0 5.5 %collective-permute-start = (bf16[8,12416]{1,0:T(8,128)(2,1)S(1)}, bf16[8,12416]{1,0:T(8,128)(2,1)S(1)}, u32[]{:S(2)}, u32[]{:S(2)}) collective-permute-start(bf16[8,12416]{1,0:T(8,128)(2,1)S(1)} %pad_maximum_fusion), channel_id=1, source_target_pairs={{0,8},{1,9},{2,10},{3,11},{4,12},{5,13},{6,14},{7,15},{8,0},{9,1},... | collective-permute-start | bytes 595976 | tf_op jit(solution)/shard_map/ppermute | solution.py:421
  10.3 1.2 copy-start
  187.3 3.3 %collective-permute-start.1 = (bf16[8,3072]{1,0:T(8,128)(2,1)S(1)}, bf16[8,3072]{1,0:T(8,128)(2,1)S(1)}, u32[]{:S(2)}, u32[]{:S(2)}) collective-permute-start(bf16[8,3072]{1,0:T(8,128)(2,1)S(1)} %get-tuple-element.9), channel_id=1, source_target_pairs={{0,8},{1,9},{2,10},{3,11},{4,12},{5,13},{6,14},{7,15},{8,0},{9,1},... | collective-permute-start | bytes 147464 | tf_op jit(solution)/shard_map/ppermute | solution.py:462

commit v4 on v3

--- a/solution.py
+++ b/solution.py
@@ -19,11 +19,12 @@
 GROUPS = ((3, 0), (0, 0), (2, 0), (3, 1), (1, 0), (2, 1), (1, 1), (0, 1))
 BEFORE = (None, None, (0, False), (1, True), (2, False), (3, False), (5, False))
 CHUNKS = 8
+THIRD = 3
 
 
 def kernel(
     raw_ref, far_ref, win_ref, wdn_ref, out_ref,
-    RAW, OUT, GOT, FAR, X, WI, WD, PRE, BACK, ES, ER, SL, PART, SUM, ARR, MIX, TURN, TS,
+    RAW, OUT, GOT, FAR, X, WI, WD, WP, PRE, BACK, ES, ER, SL, PART, SUM, ARR, MIX, TURN, TS,
     loc_sem, ws_sem, wr_sem, us_sem, ur_sem, ds_sem, dr_sem, es_sem, er_sem,
     ss_sem, sr_sem, as_sem, ar_sem, bs_sem, br_sem, ts_sem, tr_sem, ys_sem, yr_sem,
 ):
@@ -76,12 +77,18 @@
     theirs = pl.ds(pl.multiple_of((1 - xl) * half, LANES), half)
     own_raw = pltpu.make_async_copy(raw_ref, RAW.at[0], loc_sem.at[0])
     own_win = pltpu.make_async_copy(win_ref.at[:, mine], WI.at[xl], loc_sem.at[1])
-    own_wdn = pltpu.make_async_copy(wdn_ref.at[:, mine], WD.at[xl], loc_sem.at[2])
+    share = WP.shape[1]
+    my_part = pl.ds(pl.multiple_of(xl * share, LANES), share)
+    their_part = pl.ds(pl.multiple_of((1 - xl) * share, LANES), share)
+    rest = pl.ds(2 * share, share)
+    own_wdn = [
+        pltpu.make_async_copy(wdn_ref.at[:, my_part], WD.at[:, pl.ds(0, share)], loc_sem.at[2]),
+        pltpu.make_async_copy(wdn_ref.at[:, rest], WD.at[:, pl.ds(share, share)], loc_sem.at[4]),
+    ]
 
     out_win = remote(win_ref.at[:, theirs], WI.at[xl], ws_sem.at[0], wr_sem.at[0], pair)
-    out_wdn = remote(wdn_ref.at[:, theirs], WD.at[xl], ws_sem.at[1], wr_sem.at[1], pair)
+    out_wdn = remote(wdn_ref.at[:, their_part], WP, ws_sem.at[1], wr_sem.at[1], pair)
     in_win = remote(win_ref.at[:, mine], WI.at[1 - xl], ws_sem.at[0], wr_sem.at[0], pair)
-    in_wdn = remote(wdn_ref.at[:, mine], WD.at[1 - xl], ws_sem.at[1], wr_sem.at[1], pair)
 
     def to_far(j):
         e = (seat + j) % near
@@ -138,7 +145,8 @@
     far_loop(lambda c: c.start())
     out_win.start()
     own_win.start()
-    own_wdn.start()
+    for c in own_wdn:
+        c.start()
 
     size = CHUNKS * U
     slots = T // CHUNKS
@@ -174,7 +182,7 @@
         turned(GOT[r], q, at)
 
     def cols(a):
-        return pl.ds(a * half, half)
+        return pl.ds(a * (X.shape[2] // 2), X.shape[2] // 2)
 
     def up(s, a):
         src = X.at[0, pl.ds(3 * U, U), cols(a)] if s == 1 else X.at[s - 1, pl.ds(2 * U, U), cols(a)]
@@ -211,7 +219,8 @@
     raw_down(4, 1).wait_recv()
     place(4)
     own_win.wait()
-    own_wdn.wait()
+    for c in own_wdn:
+        c.wait()
     settle(0, 0, 2 * U)
 
     def project(q, at, n, h, what):
@@ -219,7 +228,9 @@
         if "p" in what:
             PRE[q, h, rows, :] = nt(X[q, rows, :half], WI[h])
         if "b" in what:
-            BACK[q, h, rows, :] = nt(X[q, rows, half:], WD[h])
+            BACK[q, h, rows, :] = nt(X[q, rows, half:], WD[...])
+        if "r" in what:
+            BACK[q, h, rows, :] = nt(X[q, rows, half : half + share], WP[...])
 
     project(0, R, R, xl, "pb")
     for s in range(1, 4):
@@ -298,14 +309,14 @@
             SUM[k, a * U : a * U + U, :] = term.astype(bf16)
             pass_on(k, a).start()
 
-    in_wdn.wait_recv()
-    project(3, 0, 2 * R, 1 - xl, "b")
+    out_wdn.wait_recv()
+    project(3, 0, 2 * R, 1 - xl, "r")
     give(0)
-    project(0, 0, 2 * R, 1 - xl, "b")
+    project(0, 0, 2 * R, 1 - xl, "r")
     give(1)
-    project(2, 0, 2 * R, 1 - xl, "b")
+    project(2, 0, 2 * R, 1 - xl, "r")
     give(2)
-    project(1, 0, 2 * R, 1 - xl, "b")
+    project(1, 0, 2 * R, 1 - xl, "r")
     add_and_pass(0)
     give(3)
     for k in range(1, 7):
@@ -374,9 +385,10 @@
             pltpu.VMEM((RING,) + far.shape, bf16),
             pltpu.VMEM((RING,) + far.shape, bf16),
             pltpu.VMEM(far.shape, bf16),
-            pltpu.VMEM((4, 2 * n_rows, width), bf16),
+            pltpu.VMEM((4, 2 * n_rows, CHUNKS * raw.shape[1]), bf16),
             pltpu.VMEM((2, hidden, half), bf16),
-            pltpu.VMEM((2, hidden, half), bf16),
+            pltpu.VMEM((hidden, 2 * width // THIRD), bf16),
+            pltpu.VMEM((hidden, width // THIRD), bf16),
             pltpu.VMEM((4, 2, 2 * n_rows, hidden), f32),
             pltpu.VMEM((4, 2, 2 * n_rows, hidden), f32),
             pltpu.VMEM((8, 2, 2, n_rows, hidden), bf16),
@@ -388,7 +400,7 @@
             pltpu.VMEM((far.shape[0], far.shape[0]), bf16),
             pltpu.VMEM(far.shape, bf16),
             pltpu.VMEM((2 * far.shape[0], back), bf16),
-            dma((4,)), dma((2,)), dma((2,)),
+            dma((5,)), dma((2,)), dma((2,)),
             dma((4, 2)), dma((4, 2)), dma((4, 2)), dma((4, 2)),
             dma((8,)), dma((8,)),
             dma((7, 2)), dma((7, 2)),
@@ -410,8 +422,14 @@
     swap = [(i, (i + RING) % blk_count) for i in range(blk_count)]
     xl = lax.axis_index("blk") // RING
 
-    def cut(a, at, side):
-        return lax.dynamic_slice(a, (0, at * width + side * half), (tok_count, half))
+    share = width // THIRD
+
+    def cut(x, dy, at, side):
+        return [
+            lax.dynamic_slice(x, (0, side * half), (tok_count, half)),
+            lax.dynamic_slice(dy, (0, at + side * share), (tok_count, share)),
+            dy[:, at + 2 * share : at + width],
+        ]
 
     small = jnp.concatenate(
         [(expert_ids * (2 * capacity) + slots + capacity * xl).astype(jnp.bfloat16), gates], axis=1
@@ -436,12 +454,9 @@
         return (same[:, :, None] * a[:, None, :]).reshape(row.shape[0], CHUNKS * n_tok).astype(jnp.bfloat16)
 
     def stacked(side):
-        rows = [
-            jnp.concatenate([cut(a, 0, side), cut(b, at, side)], axis=1)
-            for a, b, at in ((tokens, out_grad, 0), (came, came, 1))
-        ]
-        both = jnp.concatenate(rows, axis=0)
-        piece = width // CHUNKS
+        rows = [cut(tokens, out_grad, 0, side), cut(came, came, width, side)]
+        both = jnp.concatenate([jnp.concatenate(r, axis=1) for r in rows], axis=0)
+        piece = both.shape[1] // CHUNKS
         return jnp.concatenate([both[:, k * piece : (k + 1) * piece] for k in range(CHUNKS)], axis=0)
 
     near = row.shape[0] // 2

time: 193 us -> 181 us (0.938)
  Pallas kernels: 173 us -> 162 us
    pallas_call x1, Pallas kernels: 173 us -> 162 us  [expert_rows(): pl.pallas_call(kernel, out_shape=jax.ShapeDtypeStruct((2 * far.shape[0],...]
where the time goes in v4:
time: 181 us; the launch traced here: 180 us
  Pallas kernels  162 us (90%)
  local copies, waits for them, and re-layouts  4.54 us (3%)
  other arithmetic  3.77 us (2%)
  waiting for transfers between devices  3.28 us (2%)
  matrix products  2.78 us (2%)
  starting transfers between devices  2.65 us (1%)
    pallas_call x1, Pallas kernels, expert_rows(): pl.pallas_call(kernel, out_shape=jax.ShapeDtypeStruct((2 * far.shape[0],...  162 us
  transfers between devices with their start and end apart: 2, of which 2 were waited for; matrix products, arithmetic and copies ran while one was open for 1% of the time, Pallas kernels for 0%

profile of v4, /device:TPU:1, one launch (start us, length us, event | category | flops | bytes accessed | tf_op | source)
XLA Modules:
  0.0 179.7 jit_solution(7085135470753416741)
XLA Ops:
  0.6 0.8 copy.25
  1.4 0.8 copy.24
  2.2 0.8 copy.23
  2.9 0.1 fusion.23
  3.0 1.0 pad_maximum_fusion.4
  4.0 2.1 %collective-permute-start = (bf16[8,12416]{1,0:T(8,128)(2,1)S(1)}, bf16[8,12416]{1,0:T(8,128)(2,1)S(1)}, u32[]{:S(2)}, u32[]{:S(2)}) collective-permute-start(bf16[8,12416]{1,0:T(8,128)(2,1)S(1)} %pad_maximum_fusion.4), channel_id=1, source_target_pairs={{0,8},{1,9},{2,10},{3,11},{4,12},{5,13},{6,14},{7,15},{8,0},{9,1},... | collective-permute-start | bytes 595976 | tf_op jit(solution)/shard_map/ppermute | solution.py:439
  6.2 0.8 constant_dynamic-slice_fusion.2
  7.0 0.8 constant_dynamic-slice_fusion.3
  7.8 1.6 collective-permute-done
  9.4 0.1 fusion.24
  9.5 0.1 copy.26
  9.6 0.1 copy.27
  9.7 0.1 broadcast_compare_fusion
  9.8 0.1 convert_reduce_fusion.1
  10.1 0.1 copy.28
  10.2 0.1 tile.10
  10.4 0.0 copy-start
  10.4 1.3 convolution_convert_fusion.far_ref
  11.7 0.0 copy-done
  11.7 161.8 %shard_map.86 = bf16[768,512]{1,0:T(8,128)(2,1)} custom-call(bf16[144,896]{1,0:T(8,128)(2,1)} %copy-done, bf16[384,896]{1,0:T(8,128)(2,1)} %convolution_convert_fusion.far_ref, bf16[336,6144]{1,0:T(8,128)(2,1)} %bitcast.12, bf16[336,6144]{1,0:T(8,128)(2,1)} %bitcast.13), custom_call_target="tpu_custom_call" | custom-call | tf_op jit(solution)/shard_map/pallas_call | solution.py:378
  173.5 1.1 convert_reduce_fusion
  174.5 1.3 convolution_convert_fusion.1
  176.0 0.5 collective-permute-start.1
  176.6 0.2 fusion.4
  176.7 0.6 convert_element_type.66
  177.3 1.7 collective-permute-done.1
  179.0 0.7 maximum_select_fusion
  (36 shorter events, 0.4 us)
Async XLA Ops:
  4.0 5.5 %collective-permute-start = (bf16[8,12416]{1,0:T(8,128)(2,1)S(1)}, bf16[8,12416]{1,0:T(8,128)(2,1)S(1)}, u32[]{:S(2)}, u32[]{:S(2)}) collective-permute-start(bf16[8,12416]{1,0:T(8,128)(2,1)S(1)} %pad_maximum_fusion.4), channel_id=1, source_target_pairs={{0,8},{1,9},{2,10},{3,11},{4,12},{5,13},{6,14},{7,15},{8,0},{9,1},... | collective-permute-start | bytes 595976 | tf_op jit(solution)/shard_map/ppermute | solution.py:439
  10.4 1.3 copy-start
  176.0 3.0 %collective-permute-start.1 = (bf16[8,3072]{1,0:T(8,128)(2,1)S(1)}, bf16[8,3072]{1,0:T(8,128)(2,1)S(1)}, u32[]{:S(2)}, u32[]{:S(2)}) collective-permute-start(bf16[8,3072]{1,0:T(8,128)(2,1)S(1)} %get-tuple-element.10), channel_id=1, source_target_pairs={{0,8},{1,9},{2,10},{3,11},{4,12},{5,13},{6,14},{7,15},{8,0},{9,1},... | collective-permute-start | bytes 147464 | tf_op jit(solution)/shard_map/ppermute | solution.py:477

commit v5 on v4

--- a/solution.py
+++ b/solution.py
@@ -110,13 +110,15 @@
     def far_loop(body):
         lax.fori_loop(0, near, lambda j, c: (body(to_far(j)), c)[1], 0)
 
-    def to_token(j):
-        e = (me + j) % n_exp
-        a = (e // near + side) % 2
+    def to_token(a, j):
+        e = (seat + j) % near
         return remote(
-            TS.at[piece(a * near + e % near), :], out_ref.at[piece(me), :], bs_sem.at[j], br_sem.at[j],
-            {"expert": e},
+            TS.at[piece(a * near + e), :], out_ref.at[piece(me), :], bs_sem.at[a, j], br_sem.at[a, j],
+            {"expert": (side + a) % 2 * near + e},
         )
+
+    def token_loop(a, body):
+        lax.fori_loop(1 - a, near, lambda j, c: (body(to_token(a, j)), c)[1], 0)
 
     def raw_rows(a):
         return pl.ds(0, 80) if a == 0 else pl.ds(80, RAW.shape[1] - 80)
@@ -249,13 +251,14 @@
         settle(s, s, 0)
         settle(RING // 2 + s, s, 3 * U)
         project(s, 0, 2 * R, xl, "pb")
+    in_win.wait_recv()
+    for q in range(1, 4):
+        project(q, 0, 2 * R, 1 - xl, "p")
     up(4, 0).wait_recv()
     down(4, 1).wait_recv()
     settle(4, 0, 0)
     project(0, 0, R, xl, "pb")
-    in_win.wait_recv()
-    for q in range(4):
-        project(q, 0, 2 * R, 1 - xl, "p")
+    project(0, 0, 2 * R, 1 - xl, "p")
 
     def swap(k):
         return remote(ES.at[k], ER.at[k], es_sem.at[k], er_sem.at[k], pair)
@@ -270,6 +273,8 @@
     def terms(k):
         q, at = GROUPS[k][0], GROUPS[k][1] * R
         swap(k).wait_recv()
+        if k + 2 < 8:
+            give(k + 2)
         gate = jnp.zeros((R, 1), f32)
         for h in range(2):
             pre = PRE[q, h, at : at + R, :] + ER[k, 0, h].astype(f32)
@@ -315,18 +320,10 @@
     project(0, 0, 2 * R, 1 - xl, "r")
     give(1)
     project(2, 0, 2 * R, 1 - xl, "r")
-    give(2)
     project(1, 0, 2 * R, 1 - xl, "r")
-    add_and_pass(0)
-    give(3)
-    for k in range(1, 7):
+    for k in range(7):
         add_and_pass(k)
-        if k + 3 < 8:
-            give(k + 3)
     terms(7)
-
-    def send_out(j):
-        to_token(j).start()
 
     for a in range(2):
         total = (PART[a * U : a * U + U, :] + arrived(4, a) + arrived(6, 1 - a)).astype(bf16)
@@ -337,7 +334,7 @@
         TS[a * size : a * size + size, :] = jnp.dot(
             MIX[...], TURN[:, : third + LANES], preferred_element_type=f32
         ).astype(bf16)
-    expert_loop(send_out)
+        token_loop(a, lambda c: c.start())
     own_back = pltpu.make_async_copy(TS.at[piece(seat), :], out_ref.at[piece(me), :], loc_sem.at[3])
     own_back.start()
 
@@ -364,7 +361,8 @@
         for a in range(2):
             pass_on(k, a).wait_send()
     own_back.wait()
-    expert_loop(lambda j: to_token(j).wait())
+    for a in range(2):
+        token_loop(a, lambda c: c.wait())
 
 
 def expert_rows(raw, far, w_in, w_down, slots):
@@ -404,7 +402,7 @@
             dma((4, 2)), dma((4, 2)), dma((4, 2)), dma((4, 2)),
             dma((8,)), dma((8,)),
             dma((7, 2)), dma((7, 2)),
-            dma((n_exp // 2,)), dma((n_exp // 2,)), dma((n_exp,)), dma((n_exp,)),
+            dma((n_exp // 2,)), dma((n_exp // 2,)), dma((2, n_exp // 2)), dma((2, n_exp // 2)),
             dma((2, 4, 2)), dma((2, 4, 2)), dma((RING, n_exp // 2)), dma((RING, n_exp // 2)),
         ],
         compiler_params=pltpu.CompilerParams(
@@ -424,37 +422,35 @@
 
     share = width // THIRD
 
-    def cut(x, dy, at, side):
+    def cut(x, dy, side):
         return [
             lax.dynamic_slice(x, (0, side * half), (tok_count, half)),
-            lax.dynamic_slice(dy, (0, at + side * share), (tok_count, share)),
-            dy[:, at + 2 * share : at + width],
+            lax.dynamic_slice(dy, (0, side * share), (tok_count, share)),
+            dy[:, 2 * share :],
         ]
 
     small = jnp.concatenate(
-        [(expert_ids * (2 * capacity) + slots + capacity * xl).astype(jnp.bfloat16), gates], axis=1
+        [(expert_ids * (2 * capacity) + slots + capacity * xl).T.astype(jnp.bfloat16), gates.T], axis=0
     )
-    small = jnp.pad(small, ((0, 0), (0, LANES - 2 * top_count)))
-    away = jnp.concatenate([tokens, out_grad, small], axis=1)
-    came = lax.ppermute(away, "blk", swap)
-    small = jnp.concatenate([small, came[:, 2 * width :]], axis=0)
-    target = small[:, :top_count].astype(jnp.int32)
-    weight = small[:, top_count : 2 * top_count].astype(jnp.float32)
+    came = [lax.ppermute(a, "blk", swap) for a in (small, tokens, out_grad)]
+    small = jnp.concatenate([small, came[0]], axis=1)
+    target = small[:top_count].astype(jnp.int32)
+    weight = small[top_count:].astype(jnp.float32)
     slot_count = 2 * capacity
     n_tok = 2 * tok_count
     row = jnp.arange(expert_count * CHUNKS * slot_count, dtype=jnp.int32)
     row_target = row // (CHUNKS * slot_count) * slot_count + row % slot_count
     row_piece = row // slot_count % CHUNKS
     matches = (target[None] == row_target[:, None, None]).astype(jnp.float32)
-    placing = jnp.sum(matches, axis=2)
-    weighed = jnp.sum(matches * weight[None], axis=2)
+    placing = jnp.sum(matches, axis=1)
+    weighed = jnp.sum(matches * weight[None], axis=1)
     same = (row_piece[:, None] == jnp.arange(CHUNKS)[None]).astype(jnp.float32)
 
     def pieces(a):
         return (same[:, :, None] * a[:, None, :]).reshape(row.shape[0], CHUNKS * n_tok).astype(jnp.bfloat16)
 
     def stacked(side):
-        rows = [cut(tokens, out_grad, 0, side), cut(came, came, width, side)]
+        rows = [cut(tokens, out_grad, side), cut(came[1], came[2], side)]
         both = jnp.concatenate([jnp.concatenate(r, axis=1) for r in rows], axis=0)
         piece = both.shape[1] // CHUNKS
         return jnp.concatenate([both[:, k * piece : (k + 1) * piece] for k in range(CHUNKS)], axis=0)
@@ -462,7 +458,7 @@
     near = row.shape[0] // 2
     x_hi = lax.axis_index("expert") // (expert_count // 2)
     raw = stacked(xl)
-    table = jnp.tile(small[:, :top_count].T, (1, CHUNKS))
+    table = jnp.tile(small[:top_count], (1, CHUNKS))
     table = jnp.pad(table, ((0, 16 - top_count), (0, raw.shape[1] - table.shape[1])), constant_values=-1)
     raw = jnp.concatenate([raw, table], axis=0)
     far = lax.dynamic_slice(pieces(placing), ((1 - x_hi) * near, 0), (near, CHUNKS * n_tok))
@@ -479,7 +475,7 @@
         xl == 0, jnp.concatenate([own, other], axis=1), jnp.concatenate([other, own], axis=1)
     )
     first = (row_piece == 0).astype(jnp.float32) * back[:, part].astype(jnp.float32)
-    grad_gates = jnp.einsum("stk,s->tk", matches[:, :tok_count], first).astype(jnp.bfloat16)
+    grad_gates = jnp.einsum("skt,s->tk", matches[:, :, :tok_count], first).astype(jnp.bfloat16)
     return (grad_tokens, grad_gates)
 
 

time: 181 us -> 177 us (0.978)
  Pallas kernels: 162 us -> 159 us
  local copies, waits for them, and re-layouts: 4.54 us -> 1.99 us
    pallas_call x1, Pallas kernels: 162 us -> 159 us  [expert_rows(): pl.pallas_call(kernel, out_shape=jax.ShapeDtypeStruct((2 * far.shape[0],...]
    unnamed x27 -> x24, local copies, waits for them, and re-layouts: 2.49 us -> 0.21 us
  transfers between devices with their start and end apart: 2 -> 4, of which waited for: 2 -> 2; matrix products, arithmetic and copies ran while one was open for 1% -> 2% of each run, Pallas kernels for 0% -> 0%
where the time goes in v5:
time: 177 us
  Pallas kernels  159 us (90%)
  other arithmetic  4.82 us (3%)
  starting transfers between devices  3.6 us (2%)
  waiting for transfers between devices  3.59 us (2%)
  matrix products  2.77 us (2%)
  local copies, waits for them, and re-layouts  1.99 us (1%)
    pallas_call x1, Pallas kernels, expert_rows(): pl.pallas_call(kernel, out_shape=jax.ShapeDtypeStruct((2 * far.shape[0],...  159 us
  transfers between devices with their start and end apart: 4, of which 2 were waited for; matrix products, arithmetic and copies ran while one was open for 2% of the time, Pallas kernels for 0%

profile of v5, /device:TPU:1, one launch (start us, length us, event | category | flops | bytes accessed | tf_op | source)
XLA Modules:
  0.0 176.7 jit_solution(16956981279915213711)
XLA Ops:
  0.6 0.7 fusion.20
  1.4 0.7 pad_maximum_fusion.4
  2.0 2.0 %collective-permute-start = (bf16[8,8]{1,0:T(8,128)(2,1)S(1)}, bf16[8,8]{1,0:T(8,128)(2,1)S(1)}, u32[]{:S(2)}, u32[]{:S(2)}) collective-permute-start(bf16[8,8]{1,0:T(8,128)(2,1)S(1)} %pad_maximum_fusion.4), channel_id=1, source_target_pairs={{0,8},{1,9},{2,10},{3,11},{4,12},{5,13},{6,14},{7,15},{8,0},{9,1},... | collective-permute-start | bytes 392 | tf_op jit(solution)/shard_map/ppermute | solution.py:435
  4.1 0.1 collective-permute-start.2
  4.2 1.4 collective-permute-start.1
  5.6 0.8 constant_dynamic-slice_fusion.2
  6.4 0.8 constant_dynamic-slice_fusion.3
  7.3 0.0 collective-permute-done
  7.3 0.8 pad_maximum_fusion.5
  8.0 0.1 convert_reduce_fusion.1
  8.2 0.1 broadcast_compare_fusion
  8.3 0.1 tile.10
  8.4 0.0 collective-permute-done.2
  8.4 1.0 collective-permute-done.1
  9.7 0.0 copy-start
  9.7 1.2 convolution_convert_fusion.far_ref
  11.0 0.0 copy-done
  11.0 159.0 %shard_map.86 = bf16[768,512]{1,0:T(8,128)(2,1)} custom-call(bf16[144,896]{1,0:T(8,128)(2,1)} %copy-done, bf16[384,896]{1,0:T(8,128)(2,1)} %convolution_convert_fusion.far_ref, bf16[336,6144]{1,0:T(8,128)(2,1)} %bitcast.14, bf16[336,6144]{1,0:T(8,128)(2,1)} %bitcast.15), custom_call_target="tpu_custom_call" | custom-call | tf_op jit(solution)/shard_map/pallas_call | solution.py:376
  170.0 1.1 convert_reduce_fusion
  171.0 1.3 convolution_convert_fusion.1
  172.5 0.1 collective-permute-start.3
  172.6 0.2 fusion.4
  172.8 0.6 convert_bitcast_fusion
  173.4 2.6 %collective-permute-done.3 = bf16[8,3072]{1,0:T(8,128)(2,1)S(1)} collective-permute-done((bf16[8,3072]{1,0:T(8,128)(2,1)S(1)}, bf16[8,3072]{1,0:T(8,128)(2,1)S(1)}, u32[]{:S(2)}, u32[]{:S(2)}) %collective-permute-start.3) | collective-permute-done | bytes 49184 | tf_op jit(solution)/shard_map/ppermute | solution.py:473
  176.0 0.7 maximum_select_fusion
  (35 shorter events, 0.4 us)
Async XLA Ops:
  2.0 5.2 %collective-permute-start = (bf16[8,8]{1,0:T(8,128)(2,1)S(1)}, bf16[8,8]{1,0:T(8,128)(2,1)S(1)}, u32[]{:S(2)}, u32[]{:S(2)}) collective-permute-start(bf16[8,8]{1,0:T(8,128)(2,1)S(1)} %pad_maximum_fusion.4), channel_id=1, source_target_pairs={{0,8},{1,9},{2,10},{3,11},{4,12},{5,13},{6,14},{7,15},{8,0},{9,1},... | collective-permute-start | bytes 392 | tf_op jit(solution)/shard_map/ppermute | solution.py:435
  4.1 4.3 %collective-permute-start.2 = (bf16[8,6144]{1,0:T(8,128)(2,1)}, bf16[8,6144]{1,0:T(8,128)(2,1)S(1)}, u32[]{:S(2)}, u32[]{:S(2)}) collective-permute-start(bf16[8,6144]{1,0:T(8,128)(2,1)} %param.8), channel_id=1, source_target_pairs={{0,8},{1,9},{2,10},{3,11},{4,12},{5,13},{6,14},{7,15},{8,0},{9,1},... | collective-permute-start | bytes 294920 | tf_op jit(solution)/shard_map/ppermute | solution.py:435
  4.2 5.3 %collective-permute-start.1 = (bf16[8,6144]{1,0:T(8,128)(2,1)}, bf16[8,6144]{1,0:T(8,128)(2,1)S(1)}, u32[]{:S(2)}, u32[]{:S(2)}) collective-permute-start(bf16[8,6144]{1,0:T(8,128)(2,1)} %param.7), channel_id=1, source_target_pairs={{0,8},{1,9},{2,10},{3,11},{4,12},{5,13},{6,14},{7,15},{8,0},{9,1},... | collective-permute-start | bytes 294920 | tf_op jit(solution)/shard_map/ppermute | solution.py:435
  9.7 1.3 copy-start
  172.5 3.5 %collective-permute-start.3 = (bf16[8,3072]{1,0:T(8,128)(2,1)S(1)}, bf16[8,3072]{1,0:T(8,128)(2,1)S(1)}, u32[]{:S(2)}, u32[]{:S(2)}) collective-permute-start(bf16[8,3072]{1,0:T(8,128)(2,1)S(1)} %get-tuple-element.5), channel_id=1, source_target_pairs={{0,8},{1,9},{2,10},{3,11},{4,12},{5,13},{6,14},{7,15},{8,0},{9,1},... | collective-permute-start | bytes 147464 | tf_op jit(solution)/shard_map/ppermute | solution.py:473

commit v6 on v5

--- a/solution.py
+++ b/solution.py
@@ -146,6 +146,7 @@
     raw_down(1, 0).start()
     far_loop(lambda c: c.start())
     out_win.start()
+    out_wdn.start()
     own_win.start()
     for c in own_wdn:
         c.start()
@@ -246,8 +247,6 @@
         down(s, 0).wait_recv()
         if s < 3:
             down(s + 1, 0).start()
-        if s == 1:
-            out_wdn.start()
         settle(s, s, 0)
         settle(RING // 2 + s, s, 3 * U)
         project(s, 0, 2 * R, xl, "pb")

time: 177 us -> 177 us (level)
  no operation moved by 1% of the time
where the time goes in v6:
time: 177 us
  Pallas kernels  159 us (90%)
  other arithmetic  4.82 us (3%)
  starting transfers between devices  3.6 us (2%)
  waiting for transfers between devices  3.55 us (2%)
  matrix products  2.77 us (2%)
  local copies, waits for them, and re-layouts  1.99 us (1%)
    pallas_call x1, Pallas kernels, expert_rows(): pl.pallas_call(kernel, out_shape=jax.ShapeDtypeStruct((2 * far.shape[0],...  159 us
  transfers between devices with their start and end apart: 4, of which 2 were waited for; matrix products, arithmetic and copies ran while one was open for 2% of the time, Pallas kernels for 0%

profile of v6, /device:TPU:1, one launch (start us, length us, event | category | flops | bytes accessed | tf_op | source)
XLA Modules:
  0.0 176.5 jit_solution(9026524624350151877)
XLA Ops:
  0.6 0.7 fusion.20
  1.4 0.7 pad_maximum_fusion.4
  2.0 2.0 %collective-permute-start = (bf16[8,8]{1,0:T(8,128)(2,1)S(1)}, bf16[8,8]{1,0:T(8,128)(2,1)S(1)}, u32[]{:S(2)}, u32[]{:S(2)}) collective-permute-start(bf16[8,8]{1,0:T(8,128)(2,1)S(1)} %pad_maximum_fusion.4), channel_id=1, source_target_pairs={{0,8},{1,9},{2,10},{3,11},{4,12},{5,13},{6,14},{7,15},{8,0},{9,1},... | collective-permute-start | bytes 392 | tf_op jit(solution)/shard_map/ppermute | solution.py:434
  4.1 0.1 collective-permute-start.2
  4.2 1.4 collective-permute-start.1
  5.6 0.8 constant_dynamic-slice_fusion.2
  6.4 0.8 constant_dynamic-slice_fusion.3
  7.3 0.0 collective-permute-done
  7.3 0.8 pad_maximum_fusion.5
  8.0 0.1 convert_reduce_fusion.1
  8.2 0.1 broadcast_compare_fusion
  8.3 0.1 tile.10
  8.4 0.0 collective-permute-done.2
  8.4 1.0 collective-permute-done.1
  9.7 0.0 copy-start
  9.7 1.2 convolution_convert_fusion.far_ref
  11.0 0.0 copy-done
  11.0 158.9 %shard_map.86 = bf16[768,512]{1,0:T(8,128)(2,1)} custom-call(bf16[144,896]{1,0:T(8,128)(2,1)} %copy-done, bf16[384,896]{1,0:T(8,128)(2,1)} %convolution_convert_fusion.far_ref, bf16[336,6144]{1,0:T(8,128)(2,1)} %bitcast.14, bf16[336,6144]{1,0:T(8,128)(2,1)} %bitcast.15), custom_call_target="tpu_custom_call" | custom-call | tf_op jit(solution)/shard_map/pallas_call | solution.py:375
  169.9 1.1 convert_reduce_fusion
  171.0 1.3 convolution_convert_fusion.1
  172.4 0.1 collective-permute-start.3
  172.5 0.2 fusion.4
  172.7 0.6 convert_bitcast_fusion
  173.3 2.5 %collective-permute-done.3 = bf16[8,3072]{1,0:T(8,128)(2,1)S(1)} collective-permute-done((bf16[8,3072]{1,0:T(8,128)(2,1)S(1)}, bf16[8,3072]{1,0:T(8,128)(2,1)S(1)}, u32[]{:S(2)}, u32[]{:S(2)}) %collective-permute-start.3) | collective-permute-done | bytes 49184 | tf_op jit(solution)/shard_map/ppermute | solution.py:472
  175.9 0.7 maximum_select_fusion
  (35 shorter events, 0.4 us)
Async XLA Ops:
  2.0 5.2 %collective-permute-start = (bf16[8,8]{1,0:T(8,128)(2,1)S(1)}, bf16[8,8]{1,0:T(8,128)(2,1)S(1)}, u32[]{:S(2)}, u32[]{:S(2)}) collective-permute-start(bf16[8,8]{1,0:T(8,128)(2,1)S(1)} %pad_maximum_fusion.4), channel_id=1, source_target_pairs={{0,8},{1,9},{2,10},{3,11},{4,12},{5,13},{6,14},{7,15},{8,0},{9,1},... | collective-permute-start | bytes 392 | tf_op jit(solution)/shard_map/ppermute | solution.py:434
  4.1 4.3 %collective-permute-start.2 = (bf16[8,6144]{1,0:T(8,128)(2,1)}, bf16[8,6144]{1,0:T(8,128)(2,1)S(1)}, u32[]{:S(2)}, u32[]{:S(2)}) collective-permute-start(bf16[8,6144]{1,0:T(8,128)(2,1)} %param.8), channel_id=1, source_target_pairs={{0,8},{1,9},{2,10},{3,11},{4,12},{5,13},{6,14},{7,15},{8,0},{9,1},... | collective-permute-start | bytes 294920 | tf_op jit(solution)/shard_map/ppermute | solution.py:434
  4.2 5.3 %collective-permute-start.1 = (bf16[8,6144]{1,0:T(8,128)(2,1)}, bf16[8,6144]{1,0:T(8,128)(2,1)S(1)}, u32[]{:S(2)}, u32[]{:S(2)}) collective-permute-start(bf16[8,6144]{1,0:T(8,128)(2,1)} %param.7), channel_id=1, source_target_pairs={{0,8},{1,9},{2,10},{3,11},{4,12},{5,13},{6,14},{7,15},{8,0},{9,1},... | collective-permute-start | bytes 294920 | tf_op jit(solution)/shard_map/ppermute | solution.py:434
  9.7 1.3 copy-start
  172.4 3.5 %collective-permute-start.3 = (bf16[8,3072]{1,0:T(8,128)(2,1)S(1)}, bf16[8,3072]{1,0:T(8,128)(2,1)S(1)}, u32[]{:S(2)}, u32[]{:S(2)}) collective-permute-start(bf16[8,3072]{1,0:T(8,128)(2,1)S(1)} %get-tuple-element.5), channel_id=1, source_target_pairs={{0,8},{1,9},{2,10},{3,11},{4,12},{5,13},{6,14},{7,15},{8,0},{9,1},... | collective-permute-start | bytes 147464 | tf_op jit(solution)/shard_map/ppermute | solution.py:472
